TPU v7x, 256 devices: a whole 4x4x8 slice. The times are simulated.
256 devices in a mesh: chan: 16 (over x, z_lo, core), depth: 16 (over z_hi, y).
Axes of the slice: x: 4, y: 4, z: 8 (z_hi: 4, z_lo: 2; z = z_hi * 2 + z_lo), core: 2. Of those that a mesh axis runs over, the one named last changes fastest.
Arguments:
- features: bfloat16 [512, 32, 4096], P('chan', 'depth'), may hold values from -6 to 6
- kernel: bfloat16 [512, 27, 512], P('chan'), may hold values from -0.0625 to 0.0625
- cotangent: bfloat16 [512, 16, 1024], P('chan', 'depth'), may hold values from -6 to 6
Outputs:
- response: bfloat16 [512, 16, 1024], P('chan', 'depth')
- feature_grad: bfloat16 [512, 32, 4096], P('chan', 'depth')
- kernel_grad: float32 [512, 27, 512], P('chan')
All inputs are finite; a program needn't handle non-finite values.
Results may differ from a plain program's by a relative error of at most 0.001.
Values may be sent and summed in bfloat16 or wider, within the bound.
A program may use at most 128 MiB of HBM per device.

v0:
```python
import jax
import jax.numpy as jnp
from jax import lax
from jax.sharding import PartitionSpec as P

H = 64
W = 64


def shifted(value, axis, steps):
    count = lax.axis_size(axis)
    first, last = (max(0, -steps), min(count, count - steps))
    return lax.ppermute(value, axis, [(source, source + steps) for source in range(first, last)])


def extract(padded, half):
    pieces = []
    for depth_tap in range(3):
        for row_tap in range(3):
            for col_tap in range(3):
                pieces.append(
                    padded[
                        :,
                        depth_tap : depth_tap + 2 * half - 1 : 2,
                        row_tap : row_tap + H - 1 : 2,
                        col_tap : col_tap + W - 1 : 2,
                    ]
                )
    stacked = jnp.stack(pieces, axis=1)
    return stacked.reshape(padded.shape[0] * 27, half * (H // 2) * (W // 2))


def next_cell(values, axis):
    count = values.shape[axis]
    moved = lax.slice_in_dim(values, 1, count, 1, axis)
    widths = [(0, 0)] * values.ndim
    widths[axis] = (0, 1)
    return jnp.pad(moved, widths)


def on_device(features, kernel, cotangent):
    chans = features.shape[0]
    rows = features.shape[1]
    half = rows // 2
    couts = kernel.shape[2]
    cout_dev = cotangent.shape[0]
    plane_out = cotangent.shape[2]
    below = shifted(features[:, rows - 1 :, :], "depth", 1)
    above = shifted(cotangent, "depth", -1)
    slab = jnp.concatenate([below, features], axis=1).reshape(chans, rows + 1, H, W)
    padded = jnp.pad(slab, ((0, 0), (0, 0), (1, 1), (1, 1)))
    patches = extract(padded, half)
    flat_kernel = kernel.reshape(chans * 27, couts)
    contract_first = (((0,), (0,)), ((), ()))
    terms = lax.dot_general(
        flat_kernel, patches, contract_first, preferred_element_type=jnp.float32
    )
    summed = lax.psum_scatter(terms, "chan", scatter_dimension=0, tiled=True)
    response = summed.reshape(cout_dev, half, plane_out).astype(jnp.bfloat16)
    extended = jnp.concatenate([cotangent, above], axis=1)
    gathered = lax.all_gather(extended, "chan", axis=0, tiled=True)
    spread = jnp.dot(
        flat_kernel,
        gathered.reshape(couts, (half + 1) * plane_out),
        preferred_element_type=jnp.float32,
    )
    inner = gathered[:, :half, :].reshape(couts, half * plane_out)
    weight_part = lax.dot_general(
        patches, inner, (((1,), (1,)), ((), ())), preferred_element_type=jnp.float32
    )
    positions = half * lax.axis_size("depth") * plane_out
    kernel_grad = (lax.psum(weight_part, "depth") * float(positions) ** (-0.5)).reshape(
        chans, 27, couts
    )
    taps_all = spread.reshape(chans, 3, 3, 3, half + 1, H // 2, W // 2)
    depth_even = taps_all[:, 1, :, :, :half]
    depth_odd = taps_all[:, 2, :, :, :half] + taps_all[:, 0, :, :, 1:]
    by_depth = jnp.stack([depth_even, depth_odd], axis=1)
    row_even = by_depth[:, :, 1]
    row_odd = by_depth[:, :, 2] + next_cell(by_depth[:, :, 0], 4)
    by_row = jnp.stack([row_even, row_odd], axis=2)
    col_even = by_row[:, :, :, 1]
    col_odd = by_row[:, :, :, 2] + next_cell(by_row[:, :, :, 0], 5)
    by_col = jnp.stack([col_even, col_odd], axis=3)
    ordered = by_col.transpose(0, 4, 1, 5, 2, 6, 3)
    feature_grad = ordered.reshape(chans, rows, H * W).astype(jnp.bfloat16)
    return (response, feature_grad, kernel_grad)


def solution(mesh):
    in_specs = (P("chan", "depth", None), P("chan", None, None), P("chan", "depth", None))
    out_specs = (P("chan", "depth", None), P("chan", "depth", None), P("chan", None, None))
    return jax.shard_map(
        on_device, mesh=mesh, in_specs=in_specs, out_specs=out_specs, check_vma=False
    )
```

profile of v0, /device:TPU:8, one launch (start us, length us, event | category | flops | bytes accessed | tf_op | source)
XLA Modules:
  0.0 455.9 jit_solution(11120905483409518403)
XLA Ops:
  19.7 4.8 %collective-permute-done = bf16[32,1,4096]{2,1,0:T(2,128)(2,1)S(1)} collective-permute-done((bf16[32,1,4096]{2,1,0:T(2,128)(2,1)S(1)}, bf16[32,1,4096]{2,1,0:T(2,128)(2,1)S(1)}, u32[]{:S(2)}, u32[]{:S(2)}) %collective-permute-start) | collective-permute-done | bytes 262176 | tf_op jit(solution)/shard_map/ppermute | solution.py:13
  39.3 3.5 slice.157
  42.9 3.5 slice.156
  49.9 3.8 slice.154
  53.7 3.7 slice.153
  57.4 3.7 slice.152
  61.1 3.7 slice.151
  64.8 3.7 slice.150
  68.6 3.7 slice.149
  86.7 3.5 slice.175
  90.2 3.5 slice.174
  100.6 3.5 slice.171
  107.5 3.8 slice.169
  111.2 3.7 slice.168
  115.0 3.7 slice.167
  118.6 3.9 slice.166
  122.6 3.9 slice.165
  126.5 3.8 slice.164
  130.3 3.7 slice.163
  134.1 3.7 slice.162
  137.8 3.7 slice.161
  160.9 7.2 %copy.79 = bf16[32,27,1,32,32]{4,3,1,0,2:T(8,128)(2,1)} copy(bf16[32,27,1,32,32]{4,3,0,2,1:T(8,128)(2,1)} %bitcast_dynamic-update-slice_fusion) | data formatting | bytes 3538944 | tf_op jit(solution)/shard_map/stack | solution.py:29
  168.1 10.7 %reshape.37 = bf16[864,1024]{1,0:T(8,128)(2,1)} reshape(bf16[32,27,1,32,32]{4,3,1,0,2:T(8,128)(2,1)} %copy.79) | data formatting | bytes 3538944 | tf_op jit(solution)/shard_map/reshape | solution.py:30
  183.5 4.9 %copy.82 = bf16[512,2,1024]{0,2,1:T(8,128)(2,1)S(1)} copy(bf16[512,2,1024]{2,1,0:T(2,128)(2,1)} %all-gather.2.cloned.1.call-done) | data formatting | bytes 4194304 | tf_op jit(solution)/shard_map/all_gather | solution.py:61
  188.5 4.9 %convolution_bitcast_fusion = f32[864,2048]{1,0:T(8,128)} fusion(bf16[512,2048]{0,1:T(8,128)(2,1)S(1)} %bitcast.107, bf16[864,512]{1,0:T(8,128)(2,1)S(1)} %copy-done), kind=kOutput, calls=%fused_computation.9 | convolution fusion | flops 1811939328 | bytes 10059776 | tf_op jit(solution)/shard_map/dot_general | solution.py:62
  193.4 18.2 %reshape.40 = f32[32,3,3,3,2,32,32]{6,5,4,3,2,1,0:T(8,128)} reshape(f32[864,2048]{1,0:T(8,128)} %convolution_bitcast_fusion) | data formatting | bytes 14155776 | tf_op jit(solution)/shard_map/reshape | solution.py:75
  211.5 3.8 fusion.14
  215.4 10.9 %fusion.16 = (f32[32,1,3,3,1,32,32]{6,5,4,3,2,1,0:T(8,128)}, f32[32,1,3,3,1,32,32]{6,5,4,3,2,1,0:T(8,128)}, f32[32,1,3,3,1,32,32]{6,5,4,3,2,1,0:T(8,128)}) fusion(f32[32,3,3,3,2,32,32]{6,5,4,3,2,1,0:T(8,128)} %reshape.40), kind=kLoop, calls=%fused_computation.62 | loop fusion | bytes 7077888 | tf_op jit(solution)/shard_map/slice | solution.py:77
  226.3 5.1 %copy_add_fusion = f32[32,1,3,3,1,32,32]{6,5,1,0,3,4,2:T(8,128)S(1)} fusion(f32[32,1,3,3,1,32,32]{6,5,4,3,2,1,0:T(8,128)} %get-tuple-element.20, f32[32,1,3,3,1,32,32]{6,5,4,3,2,1,0:T(8,128)} %get-tuple-element.18), kind=kLoop, calls=%fused_computation.8 | loop fusion | flops 294912 | bytes 3538944 | tf_op jit(solution)/shard_map/add | solution.py:77
  236.9 5.6 %copy.87 = bf16[32,1,2,32,2,32,2]{0,6,5,4,3,2,1:T(2,128)(2,1)S(1)} copy(bf16[32,1,2,32,2,32,2]{5,3,4,2,0,1,6:T(8,128)(2,1)} %maximum_bitcast_fusion) | data formatting | bytes 1048576 | tf_op jit(solution)/shard_map/convert_element_type | solution.py:86
  244.8 22.2 %reduce-scatter.4.cloned.1.call-done = f32[32,1024]{1,0:T(8,128)} async-done(((f32[512,1024]{1,0:T(8,128)}), f32[32,1024]{1,0:T(8,128)}) %reduce-scatter.4.cloned.1.call-update) | async-done | bytes 131088
  268.8 173.6 %all-reduce.5.cloned.1.call-done = f32[864,512]{1,0:T(8,128)} async-done(((f32[864,512]{1,0:T(8,128)}), f32[864,512]{1,0:T(8,128)}) %all-reduce.5.cloned.1.call-update) | async-done | bytes 1769488 | tf_op jit(solution)/shard_map/psum | solution.py:72
  (82 shorter events, 95.7 us)
Async XLA Ops:
  7.2 17.4 %copy-start.2 = (bf16[32,2,4096]{2,1,0:T(2,128)(2,1)S(1)}, bf16[32,2,4096]{2,1,0:T(2,128)(2,1)}, u32[]{:S(2)}) copy-start(bf16[32,2,4096]{2,1,0:T(2,128)(2,1)} %param.3) | copy-start | bytes 1572868
  7.2 11.7 %copy-start.3 = (bf16[32,1,1024]{2,0,1:T(8,128)(2,1)S(1)}, bf16[32,1,1024]{2,0,1:T(8,128)(2,1)}, u32[]{:S(2)}) copy-start(bf16[32,1,1024]{2,0,1:T(8,128)(2,1)} %param.5) | copy-start | bytes 196612
  7.2 176.3 %all-gather.2.cloned.1.call-start = ((), (), s32[]{:S(2)}) async-start(), calls=%async_computation.1 | async-start | bytes 2228224 | tf_op jit(solution)/shard_map/all_gather | solution.py:61
  9.0 15.6 %collective-permute-start = (bf16[32,1,4096]{2,1,0:T(2,128)(2,1)S(1)}, bf16[32,1,4096]{2,1,0:T(2,128)(2,1)S(1)}, u32[]{:S(2)}, u32[]{:S(2)}) collective-permute-start(bf16[32,1,4096]{2,1,0:T(2,128)(2,1)S(1)} %slice.148), channel_id=1, source_target_pairs={{0,1},{1,2},{2,3},{3,4},{4,5},{5,6},{6,7},{7,8},{8,9},{9,10},{10,1... | collective-permute-start | bytes 786440 | tf_op jit(solution)/shard_map/ppermute | solution.py:13
  12.5 6.4 %collective-permute-start.1 = (bf16[32,1,1024]{2,0,1:T(8,128)(2,1)}, bf16[32,1,1024]{2,0,1:T(8,128)(2,1)S(1)}, u32[]{:S(2)}, u32[]{:S(2)}) collective-permute-start(bf16[32,1,1024]{2,0,1:T(8,128)(2,1)} %param.5), channel_id=1, source_target_pairs={{1,0},{2,1},{3,2},{4,3},{5,4},{6,5},{7,6},{8,7},{9,8},{10,9},{11,1... | collective-permute-start | bytes 196616 | tf_op jit(solution)/shard_map/ppermute | solution.py:13
  19.7 247.3 %reduce-scatter.4.cloned.1.call-start = ((), (), s32[]{:S(2)}) async-start(), calls=%async_computation.3 | async-start | bytes 2228224
  168.1 10.7 %copy-start = (bf16[864,512]{1,0:T(8,128)(2,1)S(1)}, bf16[864,512]{1,0:T(8,128)(2,1)}, u32[]{:S(2)}) copy-start(bf16[864,512]{1,0:T(8,128)(2,1)} %reshape.38) | copy-start | bytes 2654212
  183.5 259.0 %all-reduce.5.cloned.1.call-start = ((), (), s32[]{:S(2)}) async-start(), calls=%async_computation.2 | async-start | bytes 3538944 | tf_op jit(solution)/shard_map/psum | solution.py:72
  193.4 18.2 %copy-start.1 = (bf16[512,2,1024]{2,1,0:T(2,128)(2,1)S(1)}, bf16[512,2,1024]{2,1,0:T(2,128)(2,1)}, u32[]{:S(2)}) copy-start(bf16[512,2,1024]{2,1,0:T(2,128)(2,1)} %all-gather.2.cloned.1.call-done) | copy-start | bytes 6291460
  226.3 5.1 %slice-start = ((s8[4718592]{0:T(1024)(128)(4,1)}), s8[524288]{0:T(1024)(128)(4,1)S(1)}, s32[]{:S(2)}) async-start(s8[4718592]{0:T(1024)(128)(4,1)} %bitcast.105), calls=%async_computation.4 | async-start | bytes 1048576
  226.3 5.1 %slice-start.1 = ((s8[4718592]{0:T(1024)(128)(4,1)}), s8[4194304]{0:T(1024)(128)(4,1)S(1)}, s32[]{:S(2)}) async-start(s8[4718592]{0:T(1024)(128)(4,1)} %bitcast.105), calls=%async_computation.5 | async-start | bytes 8388608
Sparse Core Ops, SparseCore 0:
  19.8 42.9 all-gather.1
  183.6 83.3 reduce-scatter.3
  269.6 172.7 all-reduce.4
where the time goes:
time: 462 us; the launch traced here: 456 us
  local copies, waits for them, and re-layouts  209 us (45%)
  waiting for transfers between devices  202 us (44%)
  between operations  14.3 us (3%)
  other arithmetic  13.4 us (3%)
  matrix products  11.5 us (2%)
  starting transfers between devices  5.99 us (1%)
    psum x1, waiting for transfers between devices, on_device(): lax.psum(weight_part, 'depth') * float(positions) ** (-0.5)  174 us
    slice x27, local copies, waits for them, and re-layouts, extract(): padded[:, depth_tap:depth_tap + 2 * half - 1:2, row_tap:row_tap + H - 1:2...  97.7 us
    unnamed x44, local copies, waits for them, and re-layouts  43.1 us
    unnamed x4, waiting for transfers between devices  22.2 us
    reshape x1, local copies, waits for them, and re-layouts, on_device(): taps_all = spread.reshape(chans, 3, 3, 3, half + 1, H // 2, W // 2)  18.2 us
    slice x1, local copies, waits for them, and re-layouts, on_device(): depth_odd = taps_all[:, 2, :, :, :half] + taps_all[:, 0, :, :, 1:]  10.9 us
    reshape x1, local copies, waits for them, and re-layouts, extract(): return stacked.reshape(padded.shape[0] * 27, half * (H // 2) * (W // 2))  10.7 us
  transfers between devices with their start and end apart: 5, of which 4 were waited for; matrix products, arithmetic and copies ran while one was open for 49% of the time, Pallas kernels for 0%

commit v1 on v0

v1 whole, which is shorter than its diff:
```python
import jax
import jax.numpy as jnp
from jax import lax
from jax.experimental import pallas as pl
from jax.experimental.pallas import tpu as pltpu
from jax.sharding import PartitionSpec as P

BF16 = jnp.bfloat16
F32 = jnp.float32
MESH = pl.DeviceIdType.MESH
SPAN = 250.0
MESSAGES = 96


def near(i):
    return i + 1 - 2 * (i % 2)


def far(i):
    return 3 - i


def ring_order(half):
    return (near, far) if half == 0 else (far, near)


def bound_of(values):
    rows, lanes = values.shape
    top = jnp.max(jnp.abs(values).reshape(rows // 16, 16, lanes), axis=0)
    return jnp.maximum(top, 1e-30).astype(BF16).astype(F32)


def encode(values, bound):
    rows, lanes = values.shape
    blocks = values.reshape(rows // 16, 16, lanes)
    code = jnp.exp2(jnp.abs(blocks) * (SPAN / bound)[None] - SPAN / 2)
    return jnp.where(blocks < 0, -code, code).reshape(rows, lanes).astype(BF16)


def decode(code, bound, scale=1.0):
    rows, lanes = code.shape
    blocks = code.astype(F32).reshape(rows // 16, 16, lanes)
    size = (jnp.log2(jnp.abs(blocks)) + SPAN / 2) * (bound * (scale / SPAN))[None]
    return jnp.where(blocks < 0, -size, size).reshape(rows, lanes)


def dot(a, b, dims):
    return lax.dot_general(a, b, (dims, ((), ())), preferred_element_type=F32)


def kernel(
    feat, kern, cot, resp, fgrad, kgrad,
    perm, patches, cells_out, cells_in, gathered, terms, spread,
    part, run, sy1, ry1, sy2, ry2, sz1, rz1, sz2, rz2, codes,
    sc, rc, sx1, rx1, sx2, rx2, sz, rz, send_sem, recv_sem,
):
    chan = lax.axis_index("chan")
    depth = lax.axis_index("depth")
    x, zl, core = chan // 4, (chan // 2) % 2, chan % 2
    zh, y = depth // 4, depth % 4
    to_core = (chan + 1 - 2 * core, depth)
    to_zl = (4 * x + 2 * (1 - zl) + core, depth)
    up = (chan, (depth + 1) % 16)
    down = (chan, (depth + 15) % 16)

    def to_x(step):
        return (4 * step(x) + 2 * zl + core, depth)

    def to_y(step):
        return (chan, 4 * zh + step(y))

    def to_zh(step):
        return (chan, 4 * step(zh) + y)

    partners = (
        to_core, to_zl, up, down,
        to_x(near), to_x(far), to_y(near), to_y(far), to_zh(near), to_zh(far),
    )
    barrier = pltpu.get_barrier_semaphore()
    for partner in partners:
        pl.semaphore_signal(barrier, inc=1, device_id=partner, device_id_type=MESH)
    pl.semaphore_wait(barrier, len(partners))

    copies = []

    def send(src, dst, device):
        at = len(copies)
        copy = pltpu.make_async_remote_copy(
            src_ref=src, dst_ref=dst, send_sem=send_sem.at[at], recv_sem=recv_sem.at[at],
            device_id=device, device_id_type=MESH,
        )
        copy.start()
        copies.append(copy)
        return copy

    moves = [{}, {}]

    def gather_z(j, src):
        moves[j]["z"] = send(src, gathered.at[j, x, zl, core], to_zl)

    def gather_x(j):
        m = moves[j]
        m["z"].wait_recv()
        pair = gathered.at[j, x, :, core]
        m["near"] = send(pair, pair, to_x(near))
        m["far"] = send(pair, pair, to_x(far))
        m["own_core"] = send(pair, pair, to_core)

    def gather_opposite(j):
        m = moves[j]
        m["near"].wait_recv()
        first = gathered.at[j, near(x), :, core, 0:16]
        m["opp0"] = send(first, first, to_x(far))
        block = gathered.at[j, near(x), :, core]
        m["near_core"] = send(block, block, to_core)
        m["far"].wait_recv()
        second = gathered.at[j, far(x), :, core, 16:32]
        m["opp1"] = send(second, second, to_x(near))
        block = gathered.at[j, far(x), :, core]
        m["far_core"] = send(block, block, to_core)

    def gather_last(j):
        m = moves[j]
        m["opp0"].wait_recv()
        m["opp1"].wait_recv()
        block = gathered.at[j, near(far(x)), :, core]
        m["opp_core"] = send(block, block, to_core)

    def gather_wait(j, group):
        names = ("own_core", "near_core") if group == 0 else ("far_core", "opp_core")
        for name in names:
            moves[j][name].wait_recv()

    gathered[0, x, zl, core] = cot[...]
    gather_z(0, cot)
    halo_cot = send(cot, gathered.at[1, x, zl, core], down)

    lane_in = lax.broadcasted_iota(jnp.int32, (512, 512), 0)
    lane_out = lax.broadcasted_iota(jnp.int32, (512, 512), 1)
    target = (
        ((lane_in >> 6) & 1) * 256 + (lane_in & 1) * 128
        + (lane_in >> 7) * 32 + ((lane_in & 63) >> 1)
    )
    perm[...] = jnp.where(target == lane_out, 1.0, 0.0).astype(BF16)

    def split_cells(plane):
        rows = feat[:, plane, :]
        stacked = jnp.concatenate([rows[:, 512 * k : 512 * k + 512] for k in range(8)], axis=0)
        sorted_cells = dot(stacked, perm[...], ((1,), (0,))).astype(BF16)
        return [
            jnp.concatenate(
                [sorted_cells[32 * k : 32 * k + 32, 128 * q : 128 * q + 128] for k in range(8)],
                axis=1,
            )
            for q in range(4)
        ]

    lane = lax.broadcasted_iota(jnp.int32, (32, 1024), 1)
    not_first_col = jnp.where((lane & 31) > 0, 1.0, 0.0).astype(BF16)
    not_first_row = jnp.where(lane >= 32, 1.0, 0.0).astype(BF16)

    def right(v):
        return pltpu.roll(v, 1, 1) * not_first_col

    def lower(v):
        return pltpu.roll(v, 32, 1) * not_first_row

    def lay_patches(a, cells):
        ee, eo, oe, oo = cells
        eo_r, oo_r = right(eo), right(oo)
        rows = (
            (lower(oo_r), lower(oe), lower(oo)),
            (eo_r, ee, eo),
            (oo_r, oe, oo),
        )
        for b in range(3):
            for c in range(3):
                at = (9 * a + 3 * b + c) * 32
                patches[at : at + 32] = rows[b][c]

    odd = split_cells(1)
    for q in range(4):
        cells_out[q] = odd[q]
    halo_feat = send(cells_out, cells_in, up)
    gather_x(0)
    lay_patches(2, odd)
    lay_patches(1, split_cells(0))
    patches[864:896] = jnp.zeros((32, 1024), BF16)
    gather_opposite(0)
    halo_cot.wait_recv()
    gather_z(1, gathered.at[1, x, zl, core])
    halo_feat.wait_recv()
    has_below = jnp.where(depth > 0, 1.0, 0.0).astype(BF16)
    lay_patches(0, [cells_in[q] * has_below for q in range(4)])

    grads = {}

    def pair_at(group):
        return x // 2 if group == 0 else 1 - x // 2

    def grad_terms(g):
        weights = gathered[0, pl.ds(2 * pair_at(g), 2)].reshape(256, 1024)
        for h in (1, 0):
            first, second = ring_order(h)
            value = dot(patches[448 * h : 448 * h + 448], weights, ((1,), (1,)))
            for q in range(4):
                part[g, h, q, 0:112] = value[112 * q : 112 * q + 112]
            bound = bound_of(value)
            run[g, h] = bound
            sy1[g, h, 0:112] = encode(part[g, h, first(y), 0:112], bound)
            sy1[g, h, 112:224] = encode(part[g, h, second(first(y)), 0:112], bound)
            sy1[g, h, 224:240] = bound.astype(BF16)
            grads[g, h] = [send(sy1.at[g, h], ry1.at[g, h], to_y(first))]

    def merge_bound(g, h, other):
        bound = jnp.maximum(run[g, h], other)
        run[g, h] = bound
        return bound

    def grad_y2(g):
        for h in (1, 0):
            first, second = ring_order(h)
            grads[g, h][0].wait_recv()
            other = ry1[g, h, 224:240].astype(F32)
            bound = merge_bound(g, h, other)
            part[g, h, second(y), 0:112] += decode(ry1[g, h, 112:224], other)
            sy2[g, h, 0:112] = encode(part[g, h, second(y), 0:112], 2 * bound)
            sy2[g, h, 112:128] = bound.astype(BF16)
            grads[g, h] = [send(sy2.at[g, h], ry2.at[g, h], to_y(second))]
            part[g, h, y, 0:112] += decode(ry1[g, h, 0:112], other)

    def cells(i):
        return pl.ds(pl.multiple_of(32 * i, 32), 32)

    def grad_z1(g):
        for h in (1, 0):
            first, second = ring_order(h)
            grads[g, h][0].wait_recv()
            other = ry2[g, h, 112:128].astype(F32)
            bound = merge_bound(g, h, other)
            part[g, h, y, 0:112] += decode(ry2[g, h, 0:112], 2 * other)
            part[g, h, y, 112:128] = jnp.zeros((16, 256), F32)
            sz1[g, h, 0:32] = encode(part[g, h, y, cells(first(zh))], 4 * bound)
            sz1[g, h, 32:64] = encode(part[g, h, y, cells(second(first(zh)))], 4 * bound)
            sz1[g, h, 64:80] = bound.astype(BF16)
            grads[g, h] = [send(sz1.at[g, h], rz1.at[g, h], to_zh(first))]

    def grad_z2(g):
        for h in (1, 0):
            first, second = ring_order(h)
            grads[g, h][0].wait_recv()
            other = rz1[g, h, 64:80].astype(F32)
            bound = merge_bound(g, h, other)
            part[g, h, y, cells(second(zh))] += decode(rz1[g, h, 32:64], 4 * other)
            sz2[g, h, 0:32] = encode(part[g, h, y, cells(second(zh))], 8 * bound)
            sz2[g, h, 32:48] = bound.astype(BF16)
            grads[g, h] = [send(sz2.at[g, h], rz2.at[g, h], to_zh(second))]
            part[g, h, y, cells(zh)] += decode(rz1[g, h, 0:32], 4 * other)

    def back_z1(g):
        for h in (1, 0):
            first, second = ring_order(h)
            grads[g, h][0].wait_recv()
            other = rz2[g, h, 32:48].astype(F32)
            bound = merge_bound(g, h, other)
            total = part[g, h, y, cells(zh)] + decode(rz2[g, h, 0:32], 8 * other)
            codes[g, h, y, cells(zh)] = encode(total, 16 * bound)
            own = codes.at[g, h, y, cells(zh)]
            grads[g, h] = [send(own, own, to_zh(second)), send(own, own, to_zh(first))]

    def back_z2(g):
        for h in (1, 0):
            first, second = ring_order(h)
            grads[g, h][0].wait_recv()
            block = codes.at[g, h, y, cells(second(zh))]
            grads[g, h][0] = send(block, block, to_zh(first))

    def back_y1(g):
        for h in (1, 0):
            first, second = ring_order(h)
            grads[g, h][0].wait_recv()
            grads[g, h][1].wait_recv()
            block = codes.at[g, h, y, 0:112]
            grads[g, h] = [send(block, block, to_y(second)), send(block, block, to_y(first))]

    def back_y2(g):
        for h in (1, 0):
            first, second = ring_order(h)
            grads[g, h][0].wait_recv()
            block = codes.at[g, h, second(y), 0:112]
            grads[g, h][0] = send(block, block, to_y(first))

    def grad_result(g):
        lanes = pl.ds(pl.multiple_of(256 * pair_at(g), 256), 256)
        for h in (1, 0):
            grads[g, h][0].wait_recv()
            grads[g, h][1].wait_recv()
            for q in range(4):
                at = 448 * h + 112 * q
                count = min(112, 864 - at)
                kgrad[at : at + count, lanes] = decode(
                    codes[g, h, q, 0:count], 16 * run[g, h], 1.0 / 128
                )

    sums = {}

    def resp_terms():
        for i in range(4):
            value = dot(kern[:, 128 * i : 128 * i + 128], patches[0:864], ((0,), (0,)))
            terms[i] = value.reshape(2, 2, 32, 1024)
        bound = bound_of(terms[:, :, 1 - core].reshape(256, 1024))
        for i in range(4):
            for j in range(2):
                at = 64 * i + 32 * j
                sc[at : at + 32] = encode(terms[i, j, 1 - core], bound)
        sc[256:272] = bound.astype(BF16)
        sums["core"] = send(sc, rc, to_core)

    def resp_x1():
        sums["core"].wait_recv()
        other = rc[256:272].astype(F32)
        for i in range(4):
            for j in range(2):
                at = 64 * i + 32 * j
                terms[i, j, core] += decode(rc[at : at + 32], other)
        for h in range(2):
            first, second = ring_order(h)
            lanes = slice(512 * h, 512 * h + 512)
            blocks = [
                terms[i, j, core, :, lanes] for i in (first(x), second(first(x))) for j in range(2)
            ]
            value = jnp.concatenate(blocks, axis=0)
            bound = bound_of(value)
            sx1[h, 0:128] = encode(value, bound)
            sx1[h, 128:144] = bound.astype(BF16)
            sums["x1", h] = send(sx1.at[h], rx1.at[h], to_x(first))

    def resp_x2():
        for h in range(2):
            first, second = ring_order(h)
            lanes = slice(512 * h, 512 * h + 512)
            sums["x1", h].wait_recv()
            other = rx1[h, 128:144].astype(F32)
            for n, i in enumerate((x, second(x))):
                for j in range(2):
                    at = 64 * n + 32 * j
                    terms[i, j, core, :, lanes] += decode(rx1[h, at : at + 32], other)
            value = jnp.concatenate(
                [terms[second(x), j, core, :, lanes] for j in range(2)], axis=0
            )
            bound = bound_of(value)
            sx2[h, 0:64] = encode(value, bound)
            sx2[h, 64:80] = bound.astype(BF16)
            sums["x2", h] = send(sx2.at[h], rx2.at[h], to_x(second))

    def resp_z():
        for h in range(2):
            lanes = slice(512 * h, 512 * h + 512)
            sums["x2", h].wait_recv()
            other = rx2[h, 64:80].astype(F32)
            for j in range(2):
                terms[x, j, core, :, lanes] += decode(rx2[h, 32 * j : 32 * j + 32], other)
        value = terms[x, 1 - zl, core]
        bound = bound_of(value)
        sz[0:32] = encode(value, bound)
        sz[32:48] = bound.astype(BF16)
        sums["z"] = send(sz, rz, to_zl)

    def resp_result():
        sums["z"].wait_recv()
        total = terms[x, zl, core] + decode(rz[0:32], rz[32:48].astype(F32))
        resp[...] = total.astype(BF16)

    not_last_col = jnp.where((lane & 31) < 31, 1.0, 0.0)
    not_last_row = jnp.where(lane < 992, 1.0, 0.0)

    def left(v):
        return pltpu.roll(v, 1023, 1) * not_last_col

    def upper(v):
        return pltpu.roll(v, 992, 1) * not_last_row

    def join_cells(plane):
        def tap(b, c):
            at = (3 * b + c) * 32
            return spread[at : at + 32]

        cells = [
            tap(1, 1),
            tap(1, 2) + left(tap(1, 0)),
            tap(2, 1) + upper(tap(0, 1)),
            tap(2, 2) + left(tap(2, 0)) + upper(tap(0, 2) + left(tap(0, 0))),
        ]
        cells = [v.astype(BF16) for v in cells]
        stacked = jnp.concatenate(
            [
                jnp.concatenate([v[:, 128 * k : 128 * k + 128] for v in cells], axis=1)
                for k in range(8)
            ],
            axis=0,
        )
        rows = dot(stacked, perm[...], ((1,), (1,))).astype(BF16)
        for k in range(8):
            fgrad[32 * plane : 32 * plane + 32, 512 * k : 512 * k + 512] = rows[
                32 * k : 32 * k + 32
            ]

    def feature_even():
        cots = gathered[0].reshape(512, 1024)
        spread[...] = dot(kern[288:576], cots, ((1,), (0,)))
        join_cells(0)

    def feature_odd():
        has_above = jnp.where(depth < 15, 1.0, 0.0)
        spread[...] = dot(kern[0:288], gathered[1].reshape(512, 1024), ((1,), (0,))) * has_above
        spread[...] += dot(kern[576:864], gathered[0].reshape(512, 1024), ((1,), (0,)))
        join_cells(1)

    gather_wait(0, 0)
    grad_terms(0)
    gather_last(0)
    resp_terms()
    gather_wait(0, 1)
    grad_terms(1)
    gather_x(1)
    grad_y2(0)
    resp_x1()
    grad_y2(1)
    gather_opposite(1)
    grad_z1(0)
    resp_x2()
    grad_z1(1)
    grad_z2(0)
    gather_last(1)
    grad_z2(1)
    back_z1(0)
    resp_z()
    back_z1(1)
    back_z2(0)
    feature_even()
    back_z2(1)
    back_y1(0)
    back_y1(1)
    resp_result()
    gather_wait(1, 0)
    gather_wait(1, 1)
    feature_odd()
    back_y2(0)
    back_y2(1)
    grad_result(0)
    grad_result(1)
    for copy in copies:
        copy.wait_send()


def on_device(features, kernel_block, cotangent):
    kern = kernel_block.transpose(1, 0, 2).reshape(864, 512)
    cot = cotangent.reshape(32, 1024)
    shape = jax.ShapeDtypeStruct
    vmem = pl.BlockSpec(memory_space=pltpu.VMEM)
    resp, fgrad, kgrad = pl.pallas_call(
        kernel,
        out_shape=(shape((32, 1024), BF16), shape((64, 4096), BF16), shape((864, 512), F32)),
        in_specs=[vmem] * 3,
        out_specs=(vmem,) * 3,
        scratch_shapes=[
            pltpu.VMEM((512, 512), BF16),
            pltpu.VMEM((896, 1024), BF16),
            pltpu.VMEM((4, 32, 1024), BF16),
            pltpu.VMEM((4, 32, 1024), BF16),
            pltpu.VMEM((2, 4, 2, 2, 32, 1024), BF16),
            pltpu.VMEM((4, 2, 2, 32, 1024), F32),
            pltpu.VMEM((288, 1024), F32),
            pltpu.VMEM((2, 2, 4, 128, 256), F32),
            pltpu.VMEM((2, 2, 16, 256), F32),
        ]
        + [
            pltpu.VMEM((2, 2, rows, 256), BF16)
            for rows in (240, 240, 128, 128, 80, 80, 48, 48)
        ]
        + [
            pltpu.VMEM((2, 2, 4, 128, 256), BF16),
            pltpu.VMEM((272, 1024), BF16),
            pltpu.VMEM((272, 1024), BF16),
            pltpu.VMEM((2, 144, 512), BF16),
            pltpu.VMEM((2, 144, 512), BF16),
            pltpu.VMEM((2, 80, 512), BF16),
            pltpu.VMEM((2, 80, 512), BF16),
            pltpu.VMEM((48, 1024), BF16),
            pltpu.VMEM((48, 1024), BF16),
            pltpu.SemaphoreType.DMA((MESSAGES,)),
            pltpu.SemaphoreType.DMA((MESSAGES,)),
        ],
        compiler_params=pltpu.CompilerParams(
            collective_id=0, has_side_effects=True, vmem_limit_bytes=50 * 2**20
        ),
    )(features, kern, cot)
    return (
        resp.reshape(32, 1, 1024),
        fgrad.reshape(2, 32, 4096).transpose(1, 0, 2),
        kgrad.reshape(27, 32, 512).transpose(1, 0, 2),
    )


def solution(mesh):
    in_specs = (P("chan", "depth", None), P("chan", None, None), P("chan", "depth", None))
    out_specs = (P("chan", "depth", None), P("chan", "depth", None), P("chan", None, None))
    return jax.shard_map(
        on_device, mesh=mesh, in_specs=in_specs, out_specs=out_specs, check_vma=False
    )
```

time: 462 us -> 70 us (0.15); the launches traced: 456 us -> 69.8 us
  local copies, waits for them, and re-layouts: 209 us -> 6.21 us
  waiting for transfers between devices: 202 us -> 0 us
  Pallas kernels: 0 us -> 62.9 us
  between operations: 14.3 us -> 0.65 us
  other arithmetic: 13.4 us -> 0 us
  matrix products: 11.5 us -> 0 us
  starting transfers between devices: 5.99 us -> 0 us
    psum x1 -> x0, waiting for transfers between devices: 174 us -> none  [on_device(): lax.psum(weight_part, 'depth') * float(positions) ** (-0.5)]
    slice x31 -> x0, local copies, waits for them, and re-layouts: 111 us -> none  [the longest x27 97.7 us: extract(): padded[:, depth_tap:depth_tap + 2 * half - 1:2, row_tap:row_tap + H - 1:2...]
    pallas_call x0 -> x1, Pallas kernels: none -> 62.9 us  [on_device(): pl.pallas_call(kernel, out_shape=(shape((32, 1024), BF16), shape((64, 409...]
    unnamed x44 -> x8, local copies, waits for them, and re-layouts: 43.1 us -> 4.88 us
    reshape x5 -> x1, local copies, waits for them, and re-layouts: 33.9 us -> 1.34 us  [on_device(): fgrad.reshape(2, 32, 4096).transpose(1, 0, 2)]
    unnamed x4 -> x0, waiting for transfers between devices: 22.2 us -> none
    dot_general x3 -> x0, matrix products: 11.5 us -> none  [the longest x1 4.9 us: on_device(): jnp.dot(flat_kernel, gathered.reshape(couts, (half + 1) * plane_out), pre...]
    another operation x2 -> x0, local copies, waits for them, and re-layouts: 7.89 us -> none  [extract(): stacked = jnp.stack(pieces, axis=1)]
  transfers between devices with their start and end apart: 5 -> 0, of which waited for: 4 -> 0; matrix products, arithmetic and copies ran while one was open for 49% -> 0% of each run, Pallas kernels for 0% -> 0%
where the time goes in v1:
time: 70 us; the launch traced here: 69.8 us
  Pallas kernels  62.9 us (90%)
  local copies, waits for them, and re-layouts  6.21 us (9%)
    pallas_call x1, Pallas kernels, on_device(): pl.pallas_call(kernel, out_shape=(shape((32, 1024), BF16), shape((64, 409...  62.9 us
    unnamed x8, local copies, waits for them, and re-layouts  4.88 us

profile of v1, /device:TPU:8, one launch (start us, length us, event | category | flops | bytes accessed | tf_op | source)
XLA Modules:
  0.0 69.8 jit_solution(355037881156380373)
XLA Ops:
  0.6 0.0 copy-start
  0.6 1.2 %copy-done = bf16[32,27,512]{2,0,1:T(8,128)(2,1)S(1)} copy-done((bf16[32,27,512]{2,0,1:T(8,128)(2,1)S(1)}, bf16[32,27,512]{2,0,1:T(8,128)(2,1)}, u32[]{:S(2)}) %copy-start) | copy-done | bytes 884760
  1.8 0.0 copy-start.1
  1.8 1.0 %copy-done.1 = bf16[32,2,4096]{2,1,0:T(2,128)(2,1)S(1)} copy-done((bf16[32,2,4096]{2,1,0:T(2,128)(2,1)S(1)}, bf16[32,2,4096]{2,1,0:T(2,128)(2,1)}, u32[]{:S(2)}) %copy-start.1) | copy-done | bytes 524312
  2.8 0.0 copy-start.2
  2.8 0.8 %copy-done.2 = bf16[32,1,1024]{2,0,1:T(8,128)(2,1)S(1)} copy-done((bf16[32,1,1024]{2,0,1:T(8,128)(2,1)S(1)}, bf16[32,1,1024]{2,0,1:T(8,128)(2,1)}, u32[]{:S(2)}) %copy-start.2) | copy-done | bytes 65560
  3.7 62.9 %shard_map.58 = (bf16[32,1024]{1,0:T(8,128)(2,1)S(1)}, bf16[64,4096]{1,0:T(8,128)(2,1)S(1)}, f32[864,512]{1,0:T(8,128)S(1)}) custom-call(bf16[32,2,4096]{2,1,0:T(2,128)(2,1)S(1)} %copy-done.1, bf16[864,512]{1,0:T(8,128)(2,1)S(1)} %bitcast.13, bf16[32,1024]{1,0:T(8,128)(2,1)S(1)} %bitcast.15), custom_call_target="tpu_custom_call" | custom-call | tf_op jit(solution)/shard_map/pallas_call | solution.py:461
  66.6 1.3 %copy.8 = bf16[2,32,4096]{2,0,1:T(2,128)(2,1)} copy(bf16[2,32,4096]{2,1,0:T(8,128)(2,1)S(1)} %bitcast.14) | data formatting | bytes 1048576 | tf_op jit(solution)/shard_map/reshape | solution.py:500
  67.9 0.6 copy.11
  68.6 1.2 %copy.12 = f32[32,27,512]{2,0,1:T(8,128)} copy(f32[32,27,512]{2,0,1:T(8,128)S(1)} %bitcast.12) | data formatting | bytes 3538944
Async XLA Ops:
  0.6 1.2 %copy-start = (bf16[32,27,512]{2,0,1:T(8,128)(2,1)S(1)}, bf16[32,27,512]{2,0,1:T(8,128)(2,1)}, u32[]{:S(2)}) copy-start(bf16[32,27,512]{2,0,1:T(8,128)(2,1)} %param.4) | copy-start | bytes 2654212
  1.8 1.0 %copy-start.1 = (bf16[32,2,4096]{2,1,0:T(2,128)(2,1)S(1)}, bf16[32,2,4096]{2,1,0:T(2,128)(2,1)}, u32[]{:S(2)}) copy-start(bf16[32,2,4096]{2,1,0:T(2,128)(2,1)} %feat.1) | copy-start | bytes 1572868
  2.8 0.8 %copy-start.2 = (bf16[32,1,1024]{2,0,1:T(8,128)(2,1)S(1)}, bf16[32,1,1024]{2,0,1:T(8,128)(2,1)}, u32[]{:S(2)}) copy-start(bf16[32,1,1024]{2,0,1:T(8,128)(2,1)} %param.5) | copy-start | bytes 196612

commit v2 on v1

v2 whole, which is shorter than its diff:
```python
import jax
import jax.numpy as jnp
from jax import lax
from jax.experimental import pallas as pl
from jax.experimental.pallas import tpu as pltpu
from jax.sharding import PartitionSpec as P

BF16 = jnp.bfloat16
F32 = jnp.float32
MESH = pl.DeviceIdType.MESH
SPAN = 250.0
MESSAGES = 136
VMEM_MIB = 40


def near(i):
    return i + 1 - 2 * (i % 2)


def far(i):
    return 3 - i


def ring_order(half):
    return (near, far) if half == 0 else (far, near)


def bound_of(values):
    rows, lanes = values.shape
    top = jnp.max(jnp.abs(values).reshape(rows // 16, 16, lanes), axis=0)
    return jnp.maximum(top, 1e-30).astype(BF16).astype(F32)


def encode(values, bound):
    rows, lanes = values.shape
    blocks = values.reshape(rows // 16, 16, lanes)
    code = jnp.exp2(jnp.abs(blocks) * (SPAN / bound)[None] - SPAN / 2)
    return jnp.where(blocks < 0, -code, code).reshape(rows, lanes).astype(BF16)


def decode(code, bound, scale=1.0):
    rows, lanes = code.shape
    blocks = code.astype(F32).reshape(rows // 16, 16, lanes)
    size = (jnp.log2(jnp.abs(blocks)) + SPAN / 2) * (bound * (scale / SPAN))[None]
    return jnp.where(blocks < 0, -size, size).reshape(rows, lanes)


def dot(a, b, dims):
    return lax.dot_general(a, b, (dims, ((), ())), preferred_element_type=F32)


def kernel(
    feat_in, kern_in, cot, resp, fgrad, codes, run,
    feat, kern, perm, patches, cells_out, cells_in, gathered, terms, spread,
    part, sy1, ry1, sy2, ry2, sz1, rz1, sz2, rz2,
    sc, rc, sx1, rx1, sx2, rx2, sz, rz, local_sem, send_sem, recv_sem,
):
    chan = lax.axis_index("chan")
    depth = lax.axis_index("depth")
    x, zl, core = chan // 4, (chan // 2) % 2, chan % 2
    zh, y = depth // 4, depth % 4
    columns = (x, near(x), far(x), near(far(x)))
    to_core = (chan + 1 - 2 * core, depth)
    to_zl = (4 * x + 2 * (1 - zl) + core, depth)
    up = (chan, (depth + 1) % 16)
    down = (chan, (depth + 15) % 16)

    def opposite(i):
        return near(far(i))

    def to_x(step):
        return (4 * step(x) + 2 * zl + core, depth)

    def to_y(step):
        return (chan, 4 * zh + step(y))

    def to_zh(step):
        return (chan, 4 * step(zh) + y)

    partners = (
        to_core, to_zl, up, down, to_x(opposite),
        to_x(near), to_x(far), to_y(near), to_y(far), to_zh(near), to_zh(far),
    )
    barrier = pltpu.get_barrier_semaphore()
    for partner in partners:
        pl.semaphore_signal(barrier, inc=1, device_id=partner, device_id_type=MESH)
    load_cot = pltpu.make_async_copy(cot, gathered.at[0, x, zl, core], local_sem.at[0])
    load_feat = pltpu.make_async_copy(feat_in, feat, local_sem.at[1])
    load_kern = pltpu.make_async_copy(kern_in, kern, local_sem.at[2])
    load_cot.start()
    load_feat.start()
    load_kern.start()

    lane_in = lax.broadcasted_iota(jnp.int32, (512, 512), 0)
    lane_out = lax.broadcasted_iota(jnp.int32, (512, 512), 1)
    target = (
        ((lane_in >> 6) & 1) * 256 + (lane_in & 1) * 128
        + (lane_in >> 7) * 32 + ((lane_in & 63) >> 1)
    )
    perm[...] = jnp.where(target == lane_out, 1.0, 0.0).astype(BF16)
    pl.semaphore_wait(barrier, len(partners))

    copies = []

    def send(src, dst, device):
        at = len(copies)
        copy = pltpu.make_async_remote_copy(
            src_ref=src, dst_ref=dst, send_sem=send_sem.at[at], recv_sem=recv_sem.at[at],
            device_id=device, device_id_type=MESH,
        )
        copy.start()
        copies.append(copy)
        return copy

    sent = {}
    steps_x = (None, near, far, opposite)

    def cot_start():
        place = gathered.at[0, x, zl, core]
        sent["z"] = send(cot, place, to_zl)
        for k in (1, 2, 3):
            sent["own", k] = send(cot, place, to_x(steps_x[k]))
        sent["core", 0] = send(cot, place, to_core)
        sent["down"] = send(cot, gathered.at[1, x, zl, core], down)

    def cot_z():
        sent["z"].wait_recv()
        place = gathered.at[0, x, 1 - zl, core]
        sent["core", 4] = send(place, place, to_core)
        for k in (1, 2, 3):
            sent["other", k] = send(place, place, to_x(steps_x[k]))

    def cot_core(k):
        sent["own", k].wait_recv()
        sent["other", k].wait_recv()
        place = gathered.at[0, columns[k], :, core]
        sent["core", k] = send(place, place, to_core)

    here = set()

    def cot_wait(k):
        if k in here:
            return
        here.add(k)
        if k == 0:
            load_cot.wait()
            sent["core", 4].wait_recv()
        sent["core", k].wait_recv()

    moves = {}

    def next_z():
        sent["down"].wait_recv()
        place = gathered.at[1, x, zl, core]
        moves["z"] = send(place, place, to_zl)

    def next_x():
        moves["z"].wait_recv()
        pair = gathered.at[1, x, :, core]
        moves["near"] = send(pair, pair, to_x(near))
        moves["far"] = send(pair, pair, to_x(far))
        moves["own_core"] = send(pair, pair, to_core)

    def next_opposite():
        moves["near"].wait_recv()
        first = gathered.at[1, near(x), :, core, 0:16]
        moves["opp0"] = send(first, first, to_x(far))
        block = gathered.at[1, near(x), :, core]
        moves["near_core"] = send(block, block, to_core)
        moves["far"].wait_recv()
        second = gathered.at[1, far(x), :, core, 16:32]
        moves["opp1"] = send(second, second, to_x(near))
        block = gathered.at[1, far(x), :, core]
        moves["far_core"] = send(block, block, to_core)

    def next_last():
        moves["opp0"].wait_recv()
        moves["opp1"].wait_recv()
        block = gathered.at[1, opposite(x), :, core]
        moves["opp_core"] = send(block, block, to_core)

    def next_wait():
        for name in ("own_core", "near_core", "far_core", "opp_core"):
            moves[name].wait_recv()

    def split_cells(plane):
        rows = feat[:, plane, :]
        stacked = jnp.concatenate([rows[:, 512 * k : 512 * k + 512] for k in range(8)], axis=0)
        sorted_cells = dot(stacked, perm[...], ((1,), (0,))).astype(BF16)
        return [
            jnp.concatenate(
                [sorted_cells[32 * k : 32 * k + 32, 128 * q : 128 * q + 128] for k in range(8)],
                axis=1,
            )
            for q in range(4)
        ]

    lane = lax.broadcasted_iota(jnp.int32, (32, 1024), 1)
    not_first_col = jnp.where((lane & 31) > 0, 1.0, 0.0).astype(BF16)
    not_first_row = jnp.where(lane >= 32, 1.0, 0.0).astype(BF16)

    def right(v):
        return pltpu.roll(v, 1, 1) * not_first_col

    def lower(v):
        return pltpu.roll(v, 32, 1) * not_first_row

    def lay_patches(a, cells):
        ee, eo, oe, oo = cells
        eo_r, oo_r = right(eo), right(oo)
        rows = (
            (lower(oo_r), lower(oe), lower(oo)),
            (eo_r, ee, eo),
            (oo_r, oe, oo),
        )
        for b in range(3):
            for c in range(3):
                at = (9 * a + 3 * b + c) * 32
                patches[at : at + 32] = rows[b][c]

    def feat_odd():
        load_feat.wait()
        cells = split_cells(1)
        for q in range(4):
            cells_out[q] = cells[q]
        sent["up"] = send(cells_out, cells_in, up)
        lay_patches(2, cells)

    def feat_even():
        lay_patches(1, split_cells(0))
        patches[864:896] = jnp.zeros((32, 1024), BF16)

    def feat_below():
        sent["up"].wait_recv()
        has_below = jnp.where(depth > 0, 1.0, 0.0).astype(BF16)
        lay_patches(0, [cells_in[q] * has_below for q in range(4)])

    grads = {}

    def grad(k, h):
        first, second = ring_order(h)
        cot_wait(k)
        weights = gathered[0, columns[k]].reshape(128, 1024)
        value = dot(patches[448 * h : 448 * h + 448], weights, ((1,), (1,)))
        for q in range(4):
            part[k, h, q, 0:112] = value[112 * q : 112 * q + 112]
        bound = bound_of(value)
        run[columns[k], h] = bound
        sy1[k, h, 0:112] = encode(part[k, h, first(y), 0:112], bound)
        sy1[k, h, 112:224] = encode(part[k, h, second(first(y)), 0:112], bound)
        sy1[k, h, 224:240] = bound.astype(BF16)
        grads[k, h] = [send(sy1.at[k, h], ry1.at[k, h], to_y(first))]

    def merge_bound(k, h, other):
        bound = jnp.maximum(run[columns[k], h], other)
        run[columns[k], h] = bound
        return bound

    def y2(k, h):
        first, second = ring_order(h)
        grads[k, h][0].wait_recv()
        other = ry1[k, h, 224:240].astype(F32)
        bound = merge_bound(k, h, other)
        part[k, h, second(y), 0:112] += decode(ry1[k, h, 112:224], other)
        sy2[k, h, 0:112] = encode(part[k, h, second(y), 0:112], 2 * bound)
        sy2[k, h, 112:128] = bound.astype(BF16)
        grads[k, h] = [send(sy2.at[k, h], ry2.at[k, h], to_y(second))]
        part[k, h, y, 0:112] += decode(ry1[k, h, 0:112], other)

    def cells_at(i):
        return pl.ds(pl.multiple_of(32 * i, 32), 32)

    def z1(k, h):
        first, second = ring_order(h)
        grads[k, h][0].wait_recv()
        other = ry2[k, h, 112:128].astype(F32)
        bound = merge_bound(k, h, other)
        part[k, h, y, 0:112] += decode(ry2[k, h, 0:112], 2 * other)
        part[k, h, y, 112:128] = jnp.zeros((16, 128), F32)
        sz1[k, h, 0:32] = encode(part[k, h, y, cells_at(first(zh))], 4 * bound)
        sz1[k, h, 32:64] = encode(part[k, h, y, cells_at(second(first(zh)))], 4 * bound)
        sz1[k, h, 64:80] = bound.astype(BF16)
        grads[k, h] = [send(sz1.at[k, h], rz1.at[k, h], to_zh(first))]

    def z2(k, h):
        first, second = ring_order(h)
        grads[k, h][0].wait_recv()
        other = rz1[k, h, 64:80].astype(F32)
        bound = merge_bound(k, h, other)
        part[k, h, y, cells_at(second(zh))] += decode(rz1[k, h, 32:64], 4 * other)
        sz2[k, h, 0:32] = encode(part[k, h, y, cells_at(second(zh))], 8 * bound)
        sz2[k, h, 32:48] = bound.astype(BF16)
        grads[k, h] = [send(sz2.at[k, h], rz2.at[k, h], to_zh(second))]
        part[k, h, y, cells_at(zh)] += decode(rz1[k, h, 0:32], 4 * other)

    def back_z1(k, h):
        first, second = ring_order(h)
        grads[k, h][0].wait_recv()
        other = rz2[k, h, 32:48].astype(F32)
        bound = merge_bound(k, h, other)
        total = part[k, h, y, cells_at(zh)] + decode(rz2[k, h, 0:32], 8 * other)
        codes[columns[k], h, y, cells_at(zh)] = encode(total, 16 * bound)
        own = codes.at[columns[k], h, y, cells_at(zh)]
        grads[k, h] = [send(own, own, to_zh(second)), send(own, own, to_zh(first))]

    def back_z2(k, h):
        first, second = ring_order(h)
        grads[k, h][0].wait_recv()
        block = codes.at[columns[k], h, y, cells_at(second(zh))]
        grads[k, h][0] = send(block, block, to_zh(first))

    def back_y1(k, h):
        first, second = ring_order(h)
        grads[k, h][0].wait_recv()
        grads[k, h][1].wait_recv()
        block = codes.at[columns[k], h, y, 0:112]
        grads[k, h] = [send(block, block, to_y(second)), send(block, block, to_y(first))]

    def back_y2(k, h):
        first, second = ring_order(h)
        grads[k, h][0].wait_recv()
        block = codes.at[columns[k], h, second(y), 0:112]
        grads[k, h][0] = send(block, block, to_y(first))

    def back_wait(k, h):
        grads[k, h][0].wait_recv()
        grads[k, h][1].wait_recv()

    sums = {}

    def resp_terms(i):
        if i == 0:
            load_kern.wait()
        value = dot(kern[:, 128 * i : 128 * i + 128], patches[0:864], ((0,), (0,)))
        terms[i] = value.reshape(2, 2, 32, 1024)

    def resp_core():
        bound = bound_of(terms[:, :, 1 - core].reshape(256, 1024))
        for i in range(4):
            for j in range(2):
                at = 64 * i + 32 * j
                sc[at : at + 32] = encode(terms[i, j, 1 - core], bound)
        sc[256:272] = bound.astype(BF16)
        sums["core"] = send(sc, rc, to_core)

    def resp_x1():
        sums["core"].wait_recv()
        other = rc[256:272].astype(F32)
        for i in range(4):
            for j in range(2):
                at = 64 * i + 32 * j
                terms[i, j, core] += decode(rc[at : at + 32], other)
        for h in range(2):
            first, second = ring_order(h)
            lanes = slice(512 * h, 512 * h + 512)
            blocks = [
                terms[i, j, core, :, lanes] for i in (first(x), second(first(x))) for j in range(2)
            ]
            value = jnp.concatenate(blocks, axis=0)
            bound = bound_of(value)
            sx1[h, 0:128] = encode(value, bound)
            sx1[h, 128:144] = bound.astype(BF16)
            sums["x1", h] = send(sx1.at[h], rx1.at[h], to_x(first))

    def resp_x2():
        for h in range(2):
            first, second = ring_order(h)
            lanes = slice(512 * h, 512 * h + 512)
            sums["x1", h].wait_recv()
            other = rx1[h, 128:144].astype(F32)
            for n, i in enumerate((x, second(x))):
                for j in range(2):
                    at = 64 * n + 32 * j
                    terms[i, j, core, :, lanes] += decode(rx1[h, at : at + 32], other)
            value = jnp.concatenate(
                [terms[second(x), j, core, :, lanes] for j in range(2)], axis=0
            )
            bound = bound_of(value)
            sx2[h, 0:64] = encode(value, bound)
            sx2[h, 64:80] = bound.astype(BF16)
            sums["x2", h] = send(sx2.at[h], rx2.at[h], to_x(second))

    def resp_z():
        for h in range(2):
            lanes = slice(512 * h, 512 * h + 512)
            sums["x2", h].wait_recv()
            other = rx2[h, 64:80].astype(F32)
            for j in range(2):
                terms[x, j, core, :, lanes] += decode(rx2[h, 32 * j : 32 * j + 32], other)
        value = terms[x, 1 - zl, core]
        bound = bound_of(value)
        sz[0:32] = encode(value, bound)
        sz[32:48] = bound.astype(BF16)
        sums["z"] = send(sz, rz, to_zl)

    def resp_result():
        sums["z"].wait_recv()
        total = terms[x, zl, core] + decode(rz[0:32], rz[32:48].astype(F32))
        resp[...] = total.astype(BF16)

    not_last_col = jnp.where((lane & 31) < 31, 1.0, 0.0)
    not_last_row = jnp.where(lane < 992, 1.0, 0.0)

    def left(v):
        return pltpu.roll(v, 1023, 1) * not_last_col

    def upper(v):
        return pltpu.roll(v, 992, 1) * not_last_row

    def join_cells(plane):
        def tap(b, c):
            at = (3 * b + c) * 32
            return spread[at : at + 32]

        cells = [
            tap(1, 1),
            tap(1, 2) + left(tap(1, 0)),
            tap(2, 1) + upper(tap(0, 1)),
            tap(2, 2) + left(tap(2, 0)) + upper(tap(0, 2) + left(tap(0, 0))),
        ]
        cells = [v.astype(BF16) for v in cells]
        stacked = jnp.concatenate(
            [
                jnp.concatenate([v[:, 128 * k : 128 * k + 128] for v in cells], axis=1)
                for k in range(8)
            ],
            axis=0,
        )
        rows = dot(stacked, perm[...], ((1,), (1,))).astype(BF16)
        for k in range(8):
            fgrad[32 * plane : 32 * plane + 32, 512 * k : 512 * k + 512] = rows[
                32 * k : 32 * k + 32
            ]

    def feature_even():
        for k in range(4):
            cot_wait(k)
        cots = gathered[0].reshape(512, 1024)
        spread[...] = dot(kern[288:576], cots, ((1,), (0,)))
        join_cells(0)

    def feature_odd():
        next_wait()
        has_above = jnp.where(depth < 15, 1.0, 0.0)
        spread[...] = dot(kern[0:288], gathered[1].reshape(512, 1024), ((1,), (0,))) * has_above
        spread[...] += dot(kern[576:864], gathered[0].reshape(512, 1024), ((1,), (0,)))
        join_cells(1)

    cot_start()
    feat_odd()
    feat_even()
    cot_z()
    next_z()
    grad(0, 1)
    feat_below()
    grad(0, 0)
    cot_core(2)
    cot_core(1)
    resp_terms(0)
    resp_terms(1)
    resp_terms(2)
    resp_terms(3)
    grad(2, 1)
    grad(1, 1)
    cot_core(3)
    grad(1, 0)
    grad(2, 0)
    y2(0, 0)
    y2(0, 1)
    resp_core()
    grad(3, 0)
    grad(3, 1)
    y2(2, 1)
    next_x()
    feature_even()
    y2(1, 0)
    y2(1, 1)
    resp_x1()
    y2(2, 0)
    z1(0, 0)
    z1(0, 1)
    y2(3, 1)
    z1(1, 0)
    y2(3, 0)
    next_opposite()
    z1(2, 0)
    z1(2, 1)
    z2(0, 0)
    z1(1, 1)
    z2(0, 1)
    z1(3, 1)
    z1(3, 0)
    z2(1, 0)
    resp_x2()
    z2(2, 1)
    z2(2, 0)
    back_z1(0, 0)
    back_z1(0, 1)
    next_last()
    z2(1, 1)
    z2(3, 0)
    z2(3, 1)
    back_z1(2, 1)
    feature_odd()
    back_z1(1, 0)
    back_z1(1, 1)
    back_z1(2, 0)
    back_z2(0, 0)
    back_z2(0, 1)
    resp_z()
    back_z1(3, 1)
    back_z1(3, 0)
    back_z2(2, 1)
    back_z2(1, 0)
    back_z2(1, 1)
    back_z2(2, 0)
    back_y1(0, 1)
    back_y1(0, 0)
    back_z2(3, 1)
    back_z2(3, 0)
    resp_result()
    back_y1(2, 1)
    back_y1(1, 0)
    back_y1(1, 1)
    back_y1(2, 0)
    back_y2(0, 1)
    back_y1(3, 1)
    back_y2(0, 0)
    back_y1(3, 0)
    back_y2(2, 1)
    back_y2(1, 0)
    back_y2(1, 1)
    back_y2(2, 0)
    back_y2(3, 1)
    back_y2(3, 0)
    back_wait(0, 1)
    back_wait(0, 0)
    back_wait(1, 1)
    back_wait(1, 0)
    back_wait(2, 1)
    back_wait(2, 0)
    back_wait(3, 1)
    back_wait(3, 0)
    for copy in copies:
        copy.wait_send()


def finish(fg_in, resp_in, codes, run, fgrad, resp, kgrad, fg_v, kg_v, sem):
    copy_resp = pltpu.make_async_copy(resp_in, resp, sem.at[8])
    copy_resp.start()
    for plane in range(2):
        fg_v[:, plane, :] = fg_in[32 * plane : 32 * plane + 32]
    copy_fg = pltpu.make_async_copy(fg_v, fgrad, sem.at[9])
    copy_fg.start()
    copies = [copy_resp, copy_fg]
    for h in range(2):
        for q in range(4):
            at = 448 * h + 112 * q
            count = min(112, 864 - at)
            rows = pl.ds(at, count)
            for xb in range(4):
                kg_v[rows, 128 * xb : 128 * xb + 128] = decode(
                    codes[xb, h, q, 0:count], 16 * run[xb, h], 1.0 / 128
                )
            copy = pltpu.make_async_copy(kg_v.at[rows], kgrad.at[rows], sem.at[4 * h + q])
            copy.start()
            copies.append(copy)
    for copy in copies:
        copy.wait()


def on_device(features, kernel_block, cotangent):
    kern = kernel_block.transpose(1, 0, 2).reshape(864, 512)
    cot = cotangent.reshape(32, 1024)
    shape = jax.ShapeDtypeStruct
    vmem = pl.BlockSpec(memory_space=pltpu.VMEM)
    hbm = pl.BlockSpec(memory_space=pltpu.HBM)
    resp, fgrad, codes, run = pl.pallas_call(
        kernel,
        out_shape=(
            shape((32, 1024), BF16), shape((64, 4096), BF16),
            shape((4, 2, 4, 128, 128), BF16), shape((4, 2, 16, 128), F32),
        ),
        in_specs=[hbm] * 3,
        out_specs=(vmem,) * 4,
        scratch_shapes=[
            pltpu.VMEM((32, 2, 4096), BF16),
            pltpu.VMEM((864, 512), BF16),
            pltpu.VMEM((512, 512), BF16),
            pltpu.VMEM((896, 1024), BF16),
            pltpu.VMEM((4, 32, 1024), BF16),
            pltpu.VMEM((4, 32, 1024), BF16),
            pltpu.VMEM((2, 4, 2, 2, 32, 1024), BF16),
            pltpu.VMEM((4, 2, 2, 32, 1024), F32),
            pltpu.VMEM((288, 1024), F32),
            pltpu.VMEM((4, 2, 4, 128, 128), F32),
        ]
        + [
            pltpu.VMEM((4, 2, rows, 128), BF16)
            for rows in (240, 240, 128, 128, 80, 80, 48, 48)
        ]
        + [
            pltpu.VMEM((272, 1024), BF16),
            pltpu.VMEM((272, 1024), BF16),
            pltpu.VMEM((2, 144, 512), BF16),
            pltpu.VMEM((2, 144, 512), BF16),
            pltpu.VMEM((2, 80, 512), BF16),
            pltpu.VMEM((2, 80, 512), BF16),
            pltpu.VMEM((48, 1024), BF16),
            pltpu.VMEM((48, 1024), BF16),
            pltpu.SemaphoreType.DMA((3,)),
            pltpu.SemaphoreType.DMA((MESSAGES,)),
            pltpu.SemaphoreType.DMA((MESSAGES,)),
        ],
        compiler_params=pltpu.CompilerParams(
            collective_id=0, has_side_effects=True, vmem_limit_bytes=VMEM_MIB * 2**20
        ),
    )(features, kern, cot)
    fgrad, resp, kgrad = pl.pallas_call(
        finish,
        out_shape=(shape((32, 2, 4096), BF16), shape((32, 1024), BF16), shape((864, 512), F32)),
        in_specs=[vmem] * 4,
        out_specs=(hbm,) * 3,
        scratch_shapes=[
            pltpu.VMEM((32, 2, 4096), BF16),
            pltpu.VMEM((864, 512), F32),
            pltpu.SemaphoreType.DMA((10,)),
        ],
        compiler_params=pltpu.CompilerParams(vmem_limit_bytes=16 * 2**20),
    )(fgrad, resp, codes, run)
    return (
        resp.reshape(32, 1, 1024), fgrad, kgrad.reshape(27, 32, 512).transpose(1, 0, 2),
    )


def solution(mesh):
    in_specs = (P("chan", "depth", None), P("chan", None, None), P("chan", "depth", None))
    out_specs = (P("chan", "depth", None), P("chan", "depth", None), P("chan", None, None))
    return jax.shard_map(
        on_device, mesh=mesh, in_specs=in_specs, out_specs=out_specs, check_vma=False
    )
```

time: 70 us -> 70.2 us (level)
  Pallas kernels: 62.9 us -> 66.3 us
  local copies, waits for them, and re-layouts: 6.21 us -> 3.04 us
    unnamed x8 -> x6, local copies, waits for them, and re-layouts: 4.88 us -> 3.04 us
    pallas_call x1, Pallas kernels: 62.9 us -> 64.6 us  [on_device(): pl.pallas_call(kernel, out_shape=(shape((32, 1024), BF16), shape((64, 409...]
    pallas_call x0 -> x1, Pallas kernels: none -> 1.66 us  [on_device(): pl.pallas_call(finish, out_shape=(shape((32, 2, 4096), BF16), shape((32,...]
    reshape x1 -> x0, local copies, waits for them, and re-layouts: 1.34 us -> none  [on_device(): fgrad.reshape(2, 32, 4096).transpose(1, 0, 2)]
where the time goes in v2:
time: 70.2 us; the launch traced here: 70 us
  Pallas kernels  66.3 us (94%)
  local copies, waits for them, and re-layouts  3.04 us (4%)
    pallas_call x1, Pallas kernels, on_device(): pl.pallas_call(kernel, out_shape=(shape((32, 1024), BF16), shape((64, 409...  64.6 us
    unnamed x6, local copies, waits for them, and re-layouts  3.04 us
    pallas_call x1, Pallas kernels, on_device(): pl.pallas_call(finish, out_shape=(shape((32, 2, 4096), BF16), shape((32,...  1.66 us

profile of v2, /device:TPU:8, one launch (start us, length us, event | category | flops | bytes accessed | tf_op | source)
XLA Modules:
  0.0 70.0 jit_solution(10578518343758619826)
XLA Ops:
  0.6 0.0 copy-start
  0.6 1.2 %copy-done = bf16[32,27,512]{2,0,1:T(8,128)(2,1)S(1)} copy-done((bf16[32,27,512]{2,0,1:T(8,128)(2,1)S(1)}, bf16[32,27,512]{2,0,1:T(8,128)(2,1)}, u32[]{:S(2)}) %copy-start) | copy-done | bytes 884760
  1.8 0.0 copy-start.1
  1.8 1.0 %copy-done.1 = bf16[32,2,4096]{2,1,0:T(2,128)(2,1)S(1)} copy-done((bf16[32,2,4096]{2,1,0:T(2,128)(2,1)S(1)}, bf16[32,2,4096]{2,1,0:T(2,128)(2,1)}, u32[]{:S(2)}) %copy-start.1) | copy-done | bytes 524312
  2.8 0.0 copy-start.2
  2.8 0.8 %copy-done.2 = bf16[32,1,1024]{2,0,1:T(8,128)(2,1)S(1)} copy-done((bf16[32,1,1024]{2,0,1:T(8,128)(2,1)S(1)}, bf16[32,1,1024]{2,0,1:T(8,128)(2,1)}, u32[]{:S(2)}) %copy-start.2) | copy-done | bytes 65560
  3.7 64.6 %shard_map.58 = (bf16[32,1024]{1,0:T(8,128)(2,1)S(1)}, bf16[64,4096]{1,0:T(8,128)(2,1)S(1)}, bf16[4,2,4,128,128]{4,3,2,1,0:T(8,128)(2,1)S(1)}, f32[4,2,16,128]{3,2,1,0:T(8,128)S(1)}) custom-call(bf16[32,2,4096]{2,1,0:T(2,128)(2,1)S(1)} %copy-done.1, bf16[864,512]{1,0:T(8,128)(2,1)S(1)} %bitcast.8, bf16[32,1024]{1,0:T(8,128)(2,1)S(1)} %bitcast.9), custom_call_target="tpu_custom_call" | custom-call | tf_op jit(solution)/shard_map/pallas_call | solution.py:578
  68.3 1.7 %shard_map.59 = (bf16[32,2,4096]{2,1,0:T(2,128)(2,1)}, bf16[32,1024]{1,0:T(8,128)(2,1)}, f32[864,512]{1,0:T(8,128)}) custom-call(bf16[64,4096]{1,0:T(8,128)(2,1)S(1)} %get-tuple-element.10.fg_in, bf16[32,1024]{1,0:T(8,128)(2,1)S(1)} %get-tuple-element.11.resp_in, bf16[4,2,4,128,128]{4,3,2,1,0:T(8,128)(2,1)S(1)} %get-tuple-element.12.codes, ...), custom_call_target="tpu_custom_call" | custom-call | tf_op jit(solution)/shard_map/pallas_call | solution.py:619
Async XLA Ops:
  0.6 1.2 %copy-start = (bf16[32,27,512]{2,0,1:T(8,128)(2,1)S(1)}, bf16[32,27,512]{2,0,1:T(8,128)(2,1)}, u32[]{:S(2)}) copy-start(bf16[32,27,512]{2,0,1:T(8,128)(2,1)} %param.4) | copy-start | bytes 2654212
  1.8 1.0 %copy-start.1 = (bf16[32,2,4096]{2,1,0:T(2,128)(2,1)S(1)}, bf16[32,2,4096]{2,1,0:T(2,128)(2,1)}, u32[]{:S(2)}) copy-start(bf16[32,2,4096]{2,1,0:T(2,128)(2,1)} %feat_in.1) | copy-start | bytes 1572868
  2.8 0.8 %copy-start.2 = (bf16[32,1,1024]{2,0,1:T(8,128)(2,1)S(1)}, bf16[32,1,1024]{2,0,1:T(8,128)(2,1)}, u32[]{:S(2)}) copy-start(bf16[32,1,1024]{2,0,1:T(8,128)(2,1)} %param.5) | copy-start | bytes 196612

commit v3 on v2

--- a/solution.py
+++ b/solution.py
@@ -10,7 +10,7 @@
 MESH = pl.DeviceIdType.MESH
 SPAN = 250.0
 MESSAGES = 136
-VMEM_MIB = 40
+VMEM_MIB = 56
 
 
 def near(i):
@@ -50,10 +50,10 @@
 
 
 def kernel(
-    feat_in, kern_in, cot, resp, fgrad, codes, run,
-    feat, kern, perm, patches, cells_out, cells_in, gathered, terms, spread,
+    feat_in, kern_in, cot, resp_out, fgrad_out, codes_out, run_out,
+    resp, fgrad, codes, run, feat, kern, perm, patches, gathered, terms, spread,
     part, sy1, ry1, sy2, ry2, sz1, rz1, sz2, rz2,
-    sc, rc, sx1, rx1, sx2, rx2, sz, rz, local_sem, send_sem, recv_sem,
+    sc, rc, sx1, rx1, sx2, rx2, sz, rz, su, ru, local_sem, send_sem, recv_sem,
 ):
     chan = lax.axis_index("chan")
     depth = lax.axis_index("depth")
@@ -115,73 +115,42 @@
     sent = {}
     steps_x = (None, near, far, opposite)
 
-    def cot_start():
-        place = gathered.at[0, x, zl, core]
-        sent["z"] = send(cot, place, to_zl)
+    def cot_start(j):
+        place = gathered.at[j, x, zl, core]
+        source = place if j else cot
+        if j:
+            sent["down"].wait_recv()
+        sent[j, "z"] = send(source, place, to_zl)
+        if not j:
+            sent["down"] = send(cot, gathered.at[1, x, zl, core], down)
         for k in (1, 2, 3):
-            sent["own", k] = send(cot, place, to_x(steps_x[k]))
-        sent["core", 0] = send(cot, place, to_core)
-        sent["down"] = send(cot, gathered.at[1, x, zl, core], down)
-
-    def cot_z():
-        sent["z"].wait_recv()
-        place = gathered.at[0, x, 1 - zl, core]
-        sent["core", 4] = send(place, place, to_core)
+            sent[j, "own", k] = send(source, place, to_x(steps_x[k]))
+        sent[j, "core", 0] = send(source, place, to_core)
+
+    def cot_z(j):
+        sent[j, "z"].wait_recv()
+        place = gathered.at[j, x, 1 - zl, core]
+        sent[j, "core", 4] = send(place, place, to_core)
         for k in (1, 2, 3):
-            sent["other", k] = send(place, place, to_x(steps_x[k]))
-
-    def cot_core(k):
-        sent["own", k].wait_recv()
-        sent["other", k].wait_recv()
-        place = gathered.at[0, columns[k], :, core]
-        sent["core", k] = send(place, place, to_core)
+            sent[j, "other", k] = send(place, place, to_x(steps_x[k]))
+
+    def cot_core(j, k):
+        sent[j, "own", k].wait_recv()
+        sent[j, "other", k].wait_recv()
+        place = gathered.at[j, columns[k], :, core]
+        sent[j, "core", k] = send(place, place, to_core)
 
     here = set()
 
-    def cot_wait(k):
-        if k in here:
+    def cot_wait(j, k):
+        if (j, k) in here:
             return
-        here.add(k)
+        here.add((j, k))
         if k == 0:
-            load_cot.wait()
-            sent["core", 4].wait_recv()
-        sent["core", k].wait_recv()
-
-    moves = {}
-
-    def next_z():
-        sent["down"].wait_recv()
-        place = gathered.at[1, x, zl, core]
-        moves["z"] = send(place, place, to_zl)
-
-    def next_x():
-        moves["z"].wait_recv()
-        pair = gathered.at[1, x, :, core]
-        moves["near"] = send(pair, pair, to_x(near))
-        moves["far"] = send(pair, pair, to_x(far))
-        moves["own_core"] = send(pair, pair, to_core)
-
-    def next_opposite():
-        moves["near"].wait_recv()
-        first = gathered.at[1, near(x), :, core, 0:16]
-        moves["opp0"] = send(first, first, to_x(far))
-        block = gathered.at[1, near(x), :, core]
-        moves["near_core"] = send(block, block, to_core)
-        moves["far"].wait_recv()
-        second = gathered.at[1, far(x), :, core, 16:32]
-        moves["opp1"] = send(second, second, to_x(near))
-        block = gathered.at[1, far(x), :, core]
-        moves["far_core"] = send(block, block, to_core)
-
-    def next_last():
-        moves["opp0"].wait_recv()
-        moves["opp1"].wait_recv()
-        block = gathered.at[1, opposite(x), :, core]
-        moves["opp_core"] = send(block, block, to_core)
-
-    def next_wait():
-        for name in ("own_core", "near_core", "far_core", "opp_core"):
-            moves[name].wait_recv()
+            if j == 0:
+                load_cot.wait()
+            sent[j, "core", 4].wait_recv()
+        sent[j, "core", k].wait_recv()
 
     def split_cells(plane):
         rows = feat[:, plane, :]
@@ -221,27 +190,33 @@
     def feat_odd():
         load_feat.wait()
         cells = split_cells(1)
-        for q in range(4):
-            cells_out[q] = cells[q]
-        sent["up"] = send(cells_out, cells_in, up)
         lay_patches(2, cells)
 
     def feat_even():
         lay_patches(1, split_cells(0))
         patches[864:896] = jnp.zeros((32, 1024), BF16)
 
-    def feat_below():
-        sent["up"].wait_recv()
-        has_below = jnp.where(depth > 0, 1.0, 0.0).astype(BF16)
-        lay_patches(0, [cells_in[q] * has_below for q in range(4)])
+    has_above = jnp.where(depth < 15, 1.0, 0.0)
+    has_below = jnp.where(depth > 0, 1.0, 0.0)
 
     grads = {}
 
     def grad(k, h):
         first, second = ring_order(h)
-        cot_wait(k)
+        cot_wait(0, k)
         weights = gathered[0, columns[k]].reshape(128, 1024)
-        value = dot(patches[448 * h : 448 * h + 448], weights, ((1,), (1,)))
+        if h:
+            value = dot(patches[448:896], weights, ((1,), (1,)))
+        else:
+            cot_wait(1, k)
+            above = gathered[1, columns[k]].reshape(128, 1024)
+            value = jnp.concatenate(
+                [
+                    dot(patches[576:864], above, ((1,), (1,))) * has_above,
+                    dot(patches[288:448], weights, ((1,), (1,))),
+                ],
+                axis=0,
+            )
         for q in range(4):
             part[k, h, q, 0:112] = value[112 * q : 112 * q + 112]
         bound = bound_of(value)
@@ -325,78 +300,106 @@
     def back_wait(k, h):
         grads[k, h][0].wait_recv()
         grads[k, h][1].wait_recv()
+        keep(codes.at[columns[k], h], codes_out.at[columns[k], h])
+
+    kept = []
+
+    def keep(src, dst):
+        copy = pltpu.make_async_copy(src, dst, local_sem.at[3 + len(kept)])
+        copy.start()
+        kept.append(copy)
+
 
     sums = {}
 
-    def resp_terms(i):
-        if i == 0:
+    def resp_terms(p, i):
+        if p == 1 and i == 0:
             load_kern.wait()
-        value = dot(kern[:, 128 * i : 128 * i + 128], patches[0:864], ((0,), (0,)))
-        terms[i] = value.reshape(2, 2, 32, 1024)
-
-    def resp_core():
-        bound = bound_of(terms[:, :, 1 - core].reshape(256, 1024))
+        taps = slice(0, 288) if p else slice(288, 864)
+        rows = patches[576:864] if p else patches[288:864]
+        value = dot(kern[taps, 128 * i : 128 * i + 128], rows, ((0,), (0,)))
+        terms[p, i] = value.reshape(2, 2, 32, 1024)
+
+    def resp_core(p):
+        bound = bound_of(terms[p, :, :, 1 - core].reshape(256, 1024))
         for i in range(4):
             for j in range(2):
                 at = 64 * i + 32 * j
-                sc[at : at + 32] = encode(terms[i, j, 1 - core], bound)
-        sc[256:272] = bound.astype(BF16)
-        sums["core"] = send(sc, rc, to_core)
-
-    def resp_x1():
-        sums["core"].wait_recv()
-        other = rc[256:272].astype(F32)
+                sc[p, at : at + 32] = encode(terms[p, i, j, 1 - core], bound)
+        sc[p, 256:272] = bound.astype(BF16)
+        sums[p, 2] = send(sc.at[p], rc.at[p], to_core)
+
+    def resp_x1(p):
+        sums[p, 2].wait_recv()
+        other = rc[p, 256:272].astype(F32)
         for i in range(4):
             for j in range(2):
                 at = 64 * i + 32 * j
-                terms[i, j, core] += decode(rc[at : at + 32], other)
+                terms[p, i, j, core] += decode(rc[p, at : at + 32], other)
         for h in range(2):
             first, second = ring_order(h)
             lanes = slice(512 * h, 512 * h + 512)
             blocks = [
-                terms[i, j, core, :, lanes] for i in (first(x), second(first(x))) for j in range(2)
+                terms[p, i, j, core, :, lanes]
+                for i in (first(x), second(first(x)))
+                for j in range(2)
             ]
             value = jnp.concatenate(blocks, axis=0)
             bound = bound_of(value)
-            sx1[h, 0:128] = encode(value, bound)
-            sx1[h, 128:144] = bound.astype(BF16)
-            sums["x1", h] = send(sx1.at[h], rx1.at[h], to_x(first))
-
-    def resp_x2():
+            sx1[p, h, 0:128] = encode(value, bound)
+            sx1[p, h, 128:144] = bound.astype(BF16)
+            sums[p, h] = send(sx1.at[p, h], rx1.at[p, h], to_x(first))
+
+    def resp_x2(p):
         for h in range(2):
             first, second = ring_order(h)
             lanes = slice(512 * h, 512 * h + 512)
-            sums["x1", h].wait_recv()
-            other = rx1[h, 128:144].astype(F32)
+            sums[p, h].wait_recv()
+            other = rx1[p, h, 128:144].astype(F32)
             for n, i in enumerate((x, second(x))):
                 for j in range(2):
                     at = 64 * n + 32 * j
-                    terms[i, j, core, :, lanes] += decode(rx1[h, at : at + 32], other)
+                    terms[p, i, j, core, :, lanes] += decode(rx1[p, h, at : at + 32], other)
             value = jnp.concatenate(
-                [terms[second(x), j, core, :, lanes] for j in range(2)], axis=0
+                [terms[p, second(x), j, core, :, lanes] for j in range(2)], axis=0
             )
             bound = bound_of(value)
-            sx2[h, 0:64] = encode(value, bound)
-            sx2[h, 64:80] = bound.astype(BF16)
-            sums["x2", h] = send(sx2.at[h], rx2.at[h], to_x(second))
-
-    def resp_z():
+            sx2[p, h, 0:64] = encode(value, bound)
+            sx2[p, h, 64:80] = bound.astype(BF16)
+            sums[p, h] = send(sx2.at[p, h], rx2.at[p, h], to_x(second))
+
+    def resp_z(p):
         for h in range(2):
             lanes = slice(512 * h, 512 * h + 512)
-            sums["x2", h].wait_recv()
-            other = rx2[h, 64:80].astype(F32)
+            sums[p, h].wait_recv()
+            other = rx2[p, h, 64:80].astype(F32)
             for j in range(2):
-                terms[x, j, core, :, lanes] += decode(rx2[h, 32 * j : 32 * j + 32], other)
-        value = terms[x, 1 - zl, core]
+                terms[p, x, j, core, :, lanes] += decode(
+                    rx2[p, h, 32 * j : 32 * j + 32], other
+                )
+        value = terms[p, x, 1 - zl, core]
         bound = bound_of(value)
-        sz[0:32] = encode(value, bound)
-        sz[32:48] = bound.astype(BF16)
-        sums["z"] = send(sz, rz, to_zl)
+        sz[p, 0:32] = encode(value, bound)
+        sz[p, 32:48] = bound.astype(BF16)
+        sums[p, 2] = send(sz.at[p], rz.at[p], to_zl)
+
+    def resp_sum(p):
+        sums[p, 2].wait_recv()
+        return terms[p, x, zl, core] + decode(rz[p, 0:32], rz[p, 32:48].astype(F32))
+
+    def resp_up():
+        value = resp_sum(1)
+        bound = bound_of(value)
+        su[0:32] = encode(value, bound)
+        su[32:48] = bound.astype(BF16)
+        sums["up"] = send(su, ru, up)
 
     def resp_result():
-        sums["z"].wait_recv()
-        total = terms[x, zl, core] + decode(rz[0:32], rz[32:48].astype(F32))
+        total = resp_sum(0)
+        sums["up"].wait_recv()
+        total += decode(ru[0:32], ru[32:48].astype(F32)) * has_below
         resp[...] = total.astype(BF16)
+        keep(resp, resp_out)
 
     not_last_col = jnp.where((lane & 31) < 31, 1.0, 0.0)
     not_last_row = jnp.where(lane < 992, 1.0, 0.0)
@@ -434,104 +437,115 @@
 
     def feature_even():
         for k in range(4):
-            cot_wait(k)
+            cot_wait(0, k)
         cots = gathered[0].reshape(512, 1024)
         spread[...] = dot(kern[288:576], cots, ((1,), (0,)))
         join_cells(0)
+        keep(fgrad.at[0:32], fgrad_out.at[0:32])
 
     def feature_odd():
-        next_wait()
-        has_above = jnp.where(depth < 15, 1.0, 0.0)
+        for k in range(4):
+            cot_wait(1, k)
         spread[...] = dot(kern[0:288], gathered[1].reshape(512, 1024), ((1,), (0,))) * has_above
         spread[...] += dot(kern[576:864], gathered[0].reshape(512, 1024), ((1,), (0,)))
         join_cells(1)
-
-    cot_start()
+        keep(fgrad.at[32:64], fgrad_out.at[32:64])
+
+    cot_start(0)
     feat_odd()
     feat_even()
-    cot_z()
-    next_z()
+    resp_terms(1, 0)
+    resp_terms(1, 1)
+    resp_terms(1, 2)
+    resp_terms(1, 3)
+    resp_core(1)
+    cot_z(0)
+    resp_terms(0, 0)
+    resp_terms(0, 1)
+    resp_terms(0, 2)
+    resp_terms(0, 3)
+    cot_start(1)
+    resp_core(0)
+    resp_x1(1)
+    cot_core(0, 2)
+    cot_core(0, 1)
     grad(0, 1)
-    feat_below()
-    grad(0, 0)
-    cot_core(2)
-    cot_core(1)
-    resp_terms(0)
-    resp_terms(1)
-    resp_terms(2)
-    resp_terms(3)
+    cot_z(1)
+    resp_x1(0)
+    cot_core(0, 3)
     grad(2, 1)
     grad(1, 1)
-    cot_core(3)
-    grad(1, 0)
-    grad(2, 0)
+    grad(0, 0)
+    y2(0, 1)
+    grad(3, 1)
+    feature_even()
+    y2(2, 1)
     y2(0, 0)
-    y2(0, 1)
-    resp_core()
-    grad(3, 0)
-    grad(3, 1)
-    y2(2, 1)
-    next_x()
-    feature_even()
-    y2(1, 0)
     y2(1, 1)
-    resp_x1()
-    y2(2, 0)
+    z1(0, 1)
+    resp_x2(1)
+    z1(2, 1)
+    y2(3, 1)
     z1(0, 0)
-    z1(0, 1)
-    y2(3, 1)
-    z1(1, 0)
-    y2(3, 0)
-    next_opposite()
-    z1(2, 0)
-    z1(2, 1)
-    z2(0, 0)
+    cot_core(1, 2)
+    cot_core(1, 1)
     z1(1, 1)
     z2(0, 1)
+    grad(2, 0)
     z1(3, 1)
-    z1(3, 0)
-    z2(1, 0)
-    resp_x2()
+    grad(1, 0)
+    cot_core(1, 3)
     z2(2, 1)
-    z2(2, 0)
-    back_z1(0, 0)
+    z2(0, 0)
+    z2(1, 1)
     back_z1(0, 1)
-    next_last()
-    z2(1, 1)
-    z2(3, 0)
+    grad(3, 0)
+    feature_odd()
+    y2(2, 0)
     z2(3, 1)
     back_z1(2, 1)
-    feature_odd()
-    back_z1(1, 0)
+    y2(1, 0)
+    back_z1(0, 0)
     back_z1(1, 1)
+    resp_x2(0)
+    resp_z(1)
+    back_z2(0, 1)
+    y2(3, 0)
+    z1(2, 0)
+    back_z1(3, 1)
+    back_z2(0, 0)
+    z1(1, 0)
+    back_z2(2, 1)
+    back_y1(0, 1)
+    back_z2(1, 1)
+    z1(3, 0)
+    resp_z(0)
+    resp_up()
+    z2(2, 0)
+    back_y1(2, 1)
+    back_z2(3, 1)
+    back_y2(0, 1)
+    back_y1(0, 0)
+    back_y1(1, 1)
+    z2(1, 0)
+    back_y2(2, 1)
     back_z1(2, 0)
-    back_z2(0, 0)
-    back_z2(0, 1)
-    resp_z()
-    back_z1(3, 1)
-    back_z1(3, 0)
-    back_z2(2, 1)
-    back_z2(1, 0)
-    back_z2(1, 1)
-    back_z2(2, 0)
-    back_y1(0, 1)
-    back_y1(0, 0)
-    back_z2(3, 1)
-    back_z2(3, 0)
-    resp_result()
-    back_y1(2, 1)
-    back_y1(1, 0)
-    back_y1(1, 1)
-    back_y1(2, 0)
-    back_y2(0, 1)
+    z2(3, 0)
     back_y1(3, 1)
     back_y2(0, 0)
+    back_y2(1, 1)
+    back_z1(1, 0)
+    back_z2(2, 0)
+    back_y2(3, 1)
+    back_z1(3, 0)
+    resp_result()
+    back_z2(1, 0)
+    back_y1(2, 0)
+    back_z2(3, 0)
+    back_y1(1, 0)
+    back_y2(2, 0)
     back_y1(3, 0)
-    back_y2(2, 1)
     back_y2(1, 0)
-    back_y2(1, 1)
-    back_y2(2, 0)
-    back_y2(3, 1)
     back_y2(3, 0)
     back_wait(0, 1)
     back_wait(0, 0)
@@ -541,26 +555,40 @@
     back_wait(2, 0)
     back_wait(3, 1)
     back_wait(3, 0)
+    keep(run, run_out)
     for copy in copies:
         copy.wait_send()
-
-
-def finish(fg_in, resp_in, codes, run, fgrad, resp, kgrad, fg_v, kg_v, sem):
+    for copy in kept:
+        copy.wait()
+
+
+def finish(fg_in, resp_in, codes_in, run_in, fgrad, resp, kgrad, fg2, codes, run, fg_v, kg_v, sem):
+    loads = [
+        pltpu.make_async_copy(run_in, run, sem.at[10]),
+        pltpu.make_async_copy(fg_in, fg2, sem.at[11]),
+        pltpu.make_async_copy(codes_in.at[:, 0], codes.at[0], sem.at[12]),
+        pltpu.make_async_copy(codes_in.at[:, 1], codes.at[1], sem.at[13]),
+    ]
+    for copy in loads:
+        copy.start()
     copy_resp = pltpu.make_async_copy(resp_in, resp, sem.at[8])
     copy_resp.start()
+    loads[0].wait()
+    loads[1].wait()
     for plane in range(2):
-        fg_v[:, plane, :] = fg_in[32 * plane : 32 * plane + 32]
+        fg_v[:, plane, :] = fg2[32 * plane : 32 * plane + 32]
     copy_fg = pltpu.make_async_copy(fg_v, fgrad, sem.at[9])
     copy_fg.start()
     copies = [copy_resp, copy_fg]
     for h in range(2):
+        loads[2 + h].wait()
         for q in range(4):
             at = 448 * h + 112 * q
             count = min(112, 864 - at)
             rows = pl.ds(at, count)
             for xb in range(4):
                 kg_v[rows, 128 * xb : 128 * xb + 128] = decode(
-                    codes[xb, h, q, 0:count], 16 * run[xb, h], 1.0 / 128
+                    codes[h, xb, q, 0:count], 16 * run[xb, h], 1.0 / 128
                 )
             copy = pltpu.make_async_copy(kg_v.at[rows], kgrad.at[rows], sem.at[4 * h + q])
             copy.start()
@@ -573,7 +601,6 @@
     kern = kernel_block.transpose(1, 0, 2).reshape(864, 512)
     cot = cotangent.reshape(32, 1024)
     shape = jax.ShapeDtypeStruct
-    vmem = pl.BlockSpec(memory_space=pltpu.VMEM)
     hbm = pl.BlockSpec(memory_space=pltpu.HBM)
     resp, fgrad, codes, run = pl.pallas_call(
         kernel,
@@ -582,16 +609,18 @@
             shape((4, 2, 4, 128, 128), BF16), shape((4, 2, 16, 128), F32),
         ),
         in_specs=[hbm] * 3,
-        out_specs=(vmem,) * 4,
+        out_specs=(hbm,) * 4,
         scratch_shapes=[
+            pltpu.VMEM((32, 1024), BF16),
+            pltpu.VMEM((64, 4096), BF16),
+            pltpu.VMEM((4, 2, 4, 128, 128), BF16),
+            pltpu.VMEM((4, 2, 16, 128), F32),
             pltpu.VMEM((32, 2, 4096), BF16),
             pltpu.VMEM((864, 512), BF16),
             pltpu.VMEM((512, 512), BF16),
             pltpu.VMEM((896, 1024), BF16),
-            pltpu.VMEM((4, 32, 1024), BF16),
-            pltpu.VMEM((4, 32, 1024), BF16),
             pltpu.VMEM((2, 4, 2, 2, 32, 1024), BF16),
-            pltpu.VMEM((4, 2, 2, 32, 1024), F32),
+            pltpu.VMEM((2, 4, 2, 2, 32, 1024), F32),
             pltpu.VMEM((288, 1024), F32),
             pltpu.VMEM((4, 2, 4, 128, 128), F32),
         ]
@@ -600,15 +629,17 @@
             for rows in (240, 240, 128, 128, 80, 80, 48, 48)
         ]
         + [
-            pltpu.VMEM((272, 1024), BF16),
-            pltpu.VMEM((272, 1024), BF16),
-            pltpu.VMEM((2, 144, 512), BF16),
-            pltpu.VMEM((2, 144, 512), BF16),
-            pltpu.VMEM((2, 80, 512), BF16),
-            pltpu.VMEM((2, 80, 512), BF16),
+            pltpu.VMEM((2, 272, 1024), BF16),
+            pltpu.VMEM((2, 272, 1024), BF16),
+            pltpu.VMEM((2, 2, 144, 512), BF16),
+            pltpu.VMEM((2, 2, 144, 512), BF16),
+            pltpu.VMEM((2, 2, 80, 512), BF16),
+            pltpu.VMEM((2, 2, 80, 512), BF16),
+            pltpu.VMEM((2, 48, 1024), BF16),
+            pltpu.VMEM((2, 48, 1024), BF16),
             pltpu.VMEM((48, 1024), BF16),
             pltpu.VMEM((48, 1024), BF16),
-            pltpu.SemaphoreType.DMA((3,)),
+            pltpu.SemaphoreType.DMA((16,)),
             pltpu.SemaphoreType.DMA((MESSAGES,)),
             pltpu.SemaphoreType.DMA((MESSAGES,)),
         ],
@@ -619,14 +650,17 @@
     fgrad, resp, kgrad = pl.pallas_call(
         finish,
         out_shape=(shape((32, 2, 4096), BF16), shape((32, 1024), BF16), shape((864, 512), F32)),
-        in_specs=[vmem] * 4,
+        in_specs=[hbm] * 4,
         out_specs=(hbm,) * 3,
         scratch_shapes=[
+            pltpu.VMEM((64, 4096), BF16),
+            pltpu.VMEM((2, 4, 4, 128, 128), BF16),
+            pltpu.VMEM((4, 2, 16, 128), F32),
             pltpu.VMEM((32, 2, 4096), BF16),
             pltpu.VMEM((864, 512), F32),
-            pltpu.SemaphoreType.DMA((10,)),
+            pltpu.SemaphoreType.DMA((14,)),
         ],
-        compiler_params=pltpu.CompilerParams(vmem_limit_bytes=16 * 2**20),
+        compiler_params=pltpu.CompilerParams(vmem_limit_bytes=VMEM_MIB * 2**20),
     )(fgrad, resp, codes, run)
     return (
         resp.reshape(32, 1, 1024), fgrad, kgrad.reshape(27, 32, 512).transpose(1, 0, 2),

time: 70.2 us -> 74.1 us (1.056); the launches traced: 70 us -> 72.8 us
  Pallas kernels: 66.3 us -> 72.2 us
  local copies, waits for them, and re-layouts: 3.04 us -> 0 us
    pallas_call x1, Pallas kernels: 64.6 us -> 69 us  [on_device(): pl.pallas_call(kernel, out_shape=(shape((32, 1024), BF16), shape((64, 409...]
    unnamed x6 -> x0, local copies, waits for them, and re-layouts: 3.04 us -> none
    pallas_call x1, Pallas kernels: 1.66 us -> 3.23 us  [on_device(): pl.pallas_call(finish, out_shape=(shape((32, 2, 4096), BF16), shape((32,...]
where the time goes in v3:
time: 74.1 us; the launch traced here: 72.8 us
  Pallas kernels  72.2 us (97%)
    pallas_call x1, Pallas kernels, on_device(): pl.pallas_call(kernel, out_shape=(shape((32, 1024), BF16), shape((64, 409...  69 us
    pallas_call x1, Pallas kernels, on_device(): pl.pallas_call(finish, out_shape=(shape((32, 2, 4096), BF16), shape((32,...  3.23 us

profile of v3, /device:TPU:8, one launch (start us, length us, event | category | flops | bytes accessed | tf_op | source)
XLA Modules:
  0.0 72.8 jit_solution(16358687858289901911)
XLA Ops:
  0.6 69.0 %shard_map.58 = (bf16[32,1024]{1,0:T(8,128)(2,1)}, bf16[64,4096]{1,0:T(8,128)(2,1)}, bf16[4,2,4,128,128]{4,3,2,1,0:T(8,128)(2,1)}, f32[4,2,16,128]{3,2,1,0:T(8,128)}) custom-call(bf16[32,2,4096]{2,1,0:T(2,128)(2,1)} %feat_in.1, bf16[864,512]{1,0:T(8,128)(2,1)} %bitcast.8, bf16[32,1024]{1,0:T(8,128)(2,1)} %bitcast.9), custom_call_target="tpu_custom_call" | custom-call | tf_op jit(solution)/shard_map/pallas_call | solution.py:605
  69.6 3.2 %shard_map.59 = (bf16[32,2,4096]{2,1,0:T(2,128)(2,1)}, bf16[32,1024]{1,0:T(8,128)(2,1)}, f32[864,512]{1,0:T(8,128)}) custom-call(bf16[64,4096]{1,0:T(8,128)(2,1)} %get-tuple-element.10.fg_in, bf16[32,1024]{1,0:T(8,128)(2,1)} %get-tuple-element.11.resp_in, bf16[4,2,4,128,128]{4,3,2,1,0:T(8,128)(2,1)} %get-tuple-element.12.codes_in, ...), custom_call_target="tpu_custom_call" | custom-call | tf_op jit(solution)/shard_map/pallas_call | solution.py:650

commit v4 on v2

--- a/solution.py
+++ b/solution.py
@@ -10,7 +10,7 @@
 MESH = pl.DeviceIdType.MESH
 SPAN = 250.0
 MESSAGES = 136
-VMEM_MIB = 40
+VMEM_MIB = 56
 
 
 def near(i):
@@ -50,8 +50,8 @@
 
 
 def kernel(
-    feat_in, kern_in, cot, resp, fgrad, codes, run,
-    feat, kern, perm, patches, cells_out, cells_in, gathered, terms, spread,
+    feat_in, kern_in, cot, resp_out, fgrad_out, kgrad_out,
+    resp, fgrad, kgrad, codes, run, feat, kern, perm, patches, cells_out, cells_in, gathered, terms, spread,
     part, sy1, ry1, sy2, ry2, sz1, rz1, sz2, rz2,
     sc, rc, sx1, rx1, sx2, rx2, sz, rz, local_sem, send_sem, recv_sem,
 ):
@@ -322,9 +322,26 @@
         block = codes.at[columns[k], h, second(y), 0:112]
         grads[k, h][0] = send(block, block, to_y(first))
 
-    def back_wait(k, h):
+    kept = []
+
+    def keep(src, dst):
+        copy = pltpu.make_async_copy(src, dst, local_sem.at[3 + len(kept)])
+        copy.start()
+        kept.append(copy)
+
+    def result(k, h):
+        lanes = pl.ds(pl.multiple_of(128 * columns[k], 128), 128)
         grads[k, h][0].wait_recv()
         grads[k, h][1].wait_recv()
+        bound = 16 * run[columns[k], h]
+        for q in range(4):
+            at = 448 * h + 112 * q
+            count = min(112, 864 - at)
+            kgrad[at : at + count, lanes] = decode(
+                codes[columns[k], h, q, 0:count], bound, 1.0 / 128
+            )
+        rows = pl.ds(448 * h, 416 if h else 448)
+        keep(kgrad.at[rows, lanes], kgrad_out.at[rows, lanes])
 
     sums = {}
 
@@ -397,6 +414,7 @@
         sums["z"].wait_recv()
         total = terms[x, zl, core] + decode(rz[0:32], rz[32:48].astype(F32))
         resp[...] = total.astype(BF16)
+        keep(resp, resp_out)
 
     not_last_col = jnp.where((lane & 31) < 31, 1.0, 0.0)
     not_last_row = jnp.where(lane < 992, 1.0, 0.0)
@@ -428,9 +446,7 @@
         )
         rows = dot(stacked, perm[...], ((1,), (1,))).astype(BF16)
         for k in range(8):
-            fgrad[32 * plane : 32 * plane + 32, 512 * k : 512 * k + 512] = rows[
-                32 * k : 32 * k + 32
-            ]
+            fgrad[:, plane, 512 * k : 512 * k + 512] = rows[32 * k : 32 * k + 32]
 
     def feature_even():
         for k in range(4):
@@ -445,126 +461,117 @@
         spread[...] = dot(kern[0:288], gathered[1].reshape(512, 1024), ((1,), (0,))) * has_above
         spread[...] += dot(kern[576:864], gathered[0].reshape(512, 1024), ((1,), (0,)))
         join_cells(1)
+        keep(fgrad, fgrad_out)
 
     cot_start()
     feat_odd()
     feat_even()
     cot_z()
+    grad(0, 1)
     next_z()
-    grad(0, 1)
-    feat_below()
-    grad(0, 0)
     cot_core(2)
     cot_core(1)
+    grad(2, 1)
+    grad(1, 1)
+    cot_core(3)
+    next_x()
+    y2(0, 1)
+    grad(3, 1)
+    feat_below()
+    grad(3, 0)
+    y2(2, 1)
+    grad(0, 0)
+    z1(0, 1)
+    grad(1, 0)
+    y2(1, 1)
     resp_terms(0)
     resp_terms(1)
     resp_terms(2)
+    grad(2, 0)
+    y2(3, 0)
     resp_terms(3)
-    grad(2, 1)
-    grad(1, 1)
-    cot_core(3)
-    grad(1, 0)
-    grad(2, 0)
+    z2(0, 1)
+    resp_core()
+    feature_even()
     y2(0, 0)
-    y2(0, 1)
-    resp_core()
-    grad(3, 0)
-    grad(3, 1)
-    y2(2, 1)
-    next_x()
-    feature_even()
+    y2(3, 1)
+    next_opposite()
+    z1(3, 0)
+    z1(2, 1)
     y2(1, 0)
-    y2(1, 1)
+    back_z1(0, 1)
+    z1(1, 1)
     resp_x1()
+    z1(0, 0)
     y2(2, 0)
-    z1(0, 0)
-    z1(0, 1)
-    y2(3, 1)
     z1(1, 0)
-    y2(3, 0)
-    next_opposite()
+    next_last()
+    z2(3, 0)
+    z2(2, 1)
+    z1(3, 1)
+    back_z2(0, 1)
+    z2(1, 1)
+    z2(0, 0)
     z1(2, 0)
-    z1(2, 1)
-    z2(0, 0)
-    z1(1, 1)
-    z2(0, 1)
-    z1(3, 1)
-    z1(3, 0)
+    back_z1(3, 0)
     z2(1, 0)
+    back_z1(2, 1)
+    z2(3, 1)
     resp_x2()
-    z2(2, 1)
+    back_y1(0, 1)
+    back_z1(1, 1)
+    back_z1(0, 0)
     z2(2, 0)
-    back_z1(0, 0)
-    back_z1(0, 1)
-    next_last()
-    z2(1, 1)
-    z2(3, 0)
-    z2(3, 1)
-    back_z1(2, 1)
+    back_z2(3, 0)
+    back_z1(1, 0)
+    back_z2(2, 1)
+    back_y2(0, 1)
+    back_z1(3, 1)
+    back_z2(1, 1)
+    back_z2(0, 0)
+    resp_z()
+    back_y1(3, 0)
+    back_z1(2, 0)
     feature_odd()
-    back_z1(1, 0)
-    back_z1(1, 1)
-    back_z1(2, 0)
-    back_z2(0, 0)
-    back_z2(0, 1)
-    resp_z()
-    back_z1(3, 1)
-    back_z1(3, 0)
-    back_z2(2, 1)
-    back_z2(1, 0)
-    back_z2(1, 1)
-    back_z2(2, 0)
-    back_y1(0, 1)
+    back_y1(1, 1)
+    back_y1(2, 1)
+    result(0, 1)
+    back_y2(3, 0)
     back_y1(0, 0)
     back_z2(3, 1)
-    back_z2(3, 0)
+    back_z2(1, 0)
     resp_result()
-    back_y1(2, 1)
+    back_y2(1, 1)
+    back_z2(2, 0)
+    back_y2(2, 1)
+    back_y1(3, 1)
     back_y1(1, 0)
-    back_y1(1, 1)
+    result(3, 0)
+    back_y2(0, 0)
+    result(1, 1)
     back_y1(2, 0)
-    back_y2(0, 1)
-    back_y1(3, 1)
-    back_y2(0, 0)
-    back_y1(3, 0)
-    back_y2(2, 1)
+    result(2, 1)
+    back_y2(3, 1)
     back_y2(1, 0)
-    back_y2(1, 1)
+    result(0, 0)
     back_y2(2, 0)
-    back_y2(3, 1)
-    back_y2(3, 0)
-    back_wait(0, 1)
-    back_wait(0, 0)
-    back_wait(1, 1)
-    back_wait(1, 0)
-    back_wait(2, 1)
-    back_wait(2, 0)
-    back_wait(3, 1)
-    back_wait(3, 0)
+    result(3, 1)
+    result(1, 0)
+    result(2, 0)
     for copy in copies:
         copy.wait_send()
-
-
-def finish(fg_in, resp_in, codes, run, fgrad, resp, kgrad, fg_v, kg_v, sem):
-    copy_resp = pltpu.make_async_copy(resp_in, resp, sem.at[8])
-    copy_resp.start()
-    for plane in range(2):
-        fg_v[:, plane, :] = fg_in[32 * plane : 32 * plane + 32]
-    copy_fg = pltpu.make_async_copy(fg_v, fgrad, sem.at[9])
-    copy_fg.start()
-    copies = [copy_resp, copy_fg]
-    for h in range(2):
-        for q in range(4):
-            at = 448 * h + 112 * q
-            count = min(112, 864 - at)
-            rows = pl.ds(at, count)
-            for xb in range(4):
-                kg_v[rows, 128 * xb : 128 * xb + 128] = decode(
-                    codes[xb, h, q, 0:count], 16 * run[xb, h], 1.0 / 128
-                )
-            copy = pltpu.make_async_copy(kg_v.at[rows], kgrad.at[rows], sem.at[4 * h + q])
-            copy.start()
-            copies.append(copy)
+    for copy in kept:
+        copy.wait()
+
+
+def finish(resp_in, fgrad_in, kgrad_in, resp, fgrad, kgrad, sem):
+    copies = [
+        pltpu.make_async_copy(kgrad_in, kgrad, sem.at[0]),
+        pltpu.make_async_copy(fgrad_in, fgrad, sem.at[1]),
+        pltpu.make_async_copy(resp_in, resp, sem.at[2]),
+    ]
+    for copy in copies:
+        copy.start()
     for copy in copies:
         copy.wait()
 
@@ -573,17 +580,19 @@
     kern = kernel_block.transpose(1, 0, 2).reshape(864, 512)
     cot = cotangent.reshape(32, 1024)
     shape = jax.ShapeDtypeStruct
-    vmem = pl.BlockSpec(memory_space=pltpu.VMEM)
     hbm = pl.BlockSpec(memory_space=pltpu.HBM)
-    resp, fgrad, codes, run = pl.pallas_call(
+    results = (shape((32, 1024), BF16), shape((32, 2, 4096), BF16), shape((864, 512), F32))
+    parts = pl.pallas_call(
         kernel,
-        out_shape=(
-            shape((32, 1024), BF16), shape((64, 4096), BF16),
-            shape((4, 2, 4, 128, 128), BF16), shape((4, 2, 16, 128), F32),
-        ),
+        out_shape=results,
         in_specs=[hbm] * 3,
-        out_specs=(vmem,) * 4,
+        out_specs=(hbm,) * 3,
         scratch_shapes=[
+            pltpu.VMEM((32, 1024), BF16),
+            pltpu.VMEM((32, 2, 4096), BF16),
+            pltpu.VMEM((864, 512), F32),
+            pltpu.VMEM((4, 2, 4, 128, 128), BF16),
+            pltpu.VMEM((4, 2, 16, 128), F32),
             pltpu.VMEM((32, 2, 4096), BF16),
             pltpu.VMEM((864, 512), BF16),
             pltpu.VMEM((512, 512), BF16),
@@ -608,7 +617,7 @@
             pltpu.VMEM((2, 80, 512), BF16),
             pltpu.VMEM((48, 1024), BF16),
             pltpu.VMEM((48, 1024), BF16),
-            pltpu.SemaphoreType.DMA((3,)),
+            pltpu.SemaphoreType.DMA((16,)),
             pltpu.SemaphoreType.DMA((MESSAGES,)),
             pltpu.SemaphoreType.DMA((MESSAGES,)),
         ],
@@ -616,18 +625,14 @@
             collective_id=0, has_side_effects=True, vmem_limit_bytes=VMEM_MIB * 2**20
         ),
     )(features, kern, cot)
-    fgrad, resp, kgrad = pl.pallas_call(
+    resp, fgrad, kgrad = pl.pallas_call(
         finish,
-        out_shape=(shape((32, 2, 4096), BF16), shape((32, 1024), BF16), shape((864, 512), F32)),
-        in_specs=[vmem] * 4,
+        out_shape=results,
+        in_specs=[hbm] * 3,
         out_specs=(hbm,) * 3,
-        scratch_shapes=[
-            pltpu.VMEM((32, 2, 4096), BF16),
-            pltpu.VMEM((864, 512), F32),
-            pltpu.SemaphoreType.DMA((10,)),
-        ],
-        compiler_params=pltpu.CompilerParams(vmem_limit_bytes=16 * 2**20),
-    )(fgrad, resp, codes, run)
+        scratch_shapes=[pltpu.SemaphoreType.DMA((3,))],
+        compiler_params=pltpu.CompilerParams(vmem_limit_bytes=VMEM_MIB * 2**20),
+    )(*parts)
     return (
         resp.reshape(32, 1, 1024), fgrad, kgrad.reshape(27, 32, 512).transpose(1, 0, 2),
     )

time: 70.2 us -> 139 us (1.98)
  Pallas kernels: 66.3 us -> 137 us
  local copies, waits for them, and re-layouts: 3.04 us -> 0 us
    pallas_call x2, Pallas kernels: 66.3 us -> 137 us  [the longest x1 72.6 us: on_device(): pl.pallas_call(finish, out_shape=results, in_specs=[hbm] * 3, out_specs=(...]
    unnamed x6 -> x0, local copies, waits for them, and re-layouts: 3.04 us -> none
where the time goes in v4:
time: 139 us; the launch traced here: 138 us
  Pallas kernels  137 us (99%)
    pallas_call x1, Pallas kernels, on_device(): pl.pallas_call(finish, out_shape=results, in_specs=[hbm] * 3, out_specs=(...  72.6 us
    pallas_call x1, Pallas kernels, on_device(): pl.pallas_call(kernel, out_shape=results, in_specs=[hbm] * 3, out_specs=(...  64.6 us

profile of v4, /device:TPU:8, one launch (start us, length us, event | category | flops | bytes accessed | tf_op | source)
XLA Modules:
  0.0 137.9 jit_solution(7739188054608941628)
XLA Ops:
  0.6 64.6 %shard_map.58 = (bf16[32,1024]{1,0:T(8,128)(2,1)}, bf16[32,2,4096]{2,1,0:T(2,128)(2,1)}, f32[864,512]{1,0:T(8,128)}) custom-call(bf16[32,2,4096]{2,1,0:T(2,128)(2,1)} %feat_in.1, bf16[864,512]{1,0:T(8,128)(2,1)} %bitcast.8, bf16[32,1024]{1,0:T(8,128)(2,1)} %bitcast.9), custom_call_target="tpu_custom_call" | custom-call | tf_op jit(solution)/shard_map/pallas_call | solution.py:585
  65.3 72.6 %shard_map.59 = (bf16[32,1024]{1,0:T(8,128)(2,1)}, bf16[32,2,4096]{2,1,0:T(2,128)(2,1)}, f32[864,512]{1,0:T(8,128)}) custom-call(bf16[32,1024]{1,0:T(8,128)(2,1)} %get-tuple-element.9.resp_in, bf16[32,2,4096]{2,1,0:T(2,128)(2,1)} %get-tuple-element.10.fgrad_in, f32[864,512]{1,0:T(8,128)} %get-tuple-element.11.kgrad_in), custom_call_target="tpu_custom_call" | custom-call | tf_op jit(solution)/shard_map/pallas_call | solution.py:628

commit v5 on v4

--- a/solution.py
+++ b/solution.py
@@ -474,89 +474,89 @@
     grad(2, 1)
     grad(1, 1)
     cot_core(3)
-    next_x()
     y2(0, 1)
     grad(3, 1)
+    next_x()
     feat_below()
+    grad(1, 0)
+    grad(0, 0)
     grad(3, 0)
+    y2(1, 1)
+    z1(0, 1)
+    grad(2, 0)
     y2(2, 1)
-    grad(0, 0)
-    z1(0, 1)
-    grad(1, 0)
-    y2(1, 1)
     resp_terms(0)
+    y2(3, 1)
     resp_terms(1)
+    y2(1, 0)
     resp_terms(2)
-    grad(2, 0)
+    next_opposite()
+    resp_terms(3)
+    y2(0, 0)
+    z2(0, 1)
+    feature_even()
+    z1(1, 0)
     y2(3, 0)
-    resp_terms(3)
-    z2(0, 1)
+    z1(1, 1)
+    z1(0, 0)
+    next_last()
+    back_z1(0, 1)
+    y2(2, 0)
     resp_core()
-    feature_even()
-    y2(0, 0)
-    y2(3, 1)
-    next_opposite()
     z1(3, 0)
     z1(2, 1)
-    y2(1, 0)
-    back_z1(0, 1)
-    z1(1, 1)
-    resp_x1()
-    z1(0, 0)
-    y2(2, 0)
-    z1(1, 0)
-    next_last()
-    z2(3, 0)
-    z2(2, 1)
+    z2(1, 0)
     z1(3, 1)
-    back_z2(0, 1)
     z2(1, 1)
     z2(0, 0)
+    back_z2(0, 1)
     z1(2, 0)
+    resp_x1()
+    z2(2, 1)
+    z2(3, 0)
+    back_z1(1, 1)
+    back_z1(1, 0)
+    z2(3, 1)
+    z2(2, 0)
+    back_z1(0, 0)
+    back_y1(0, 1)
+    back_z1(2, 1)
     back_z1(3, 0)
-    z2(1, 0)
-    back_z1(2, 1)
-    z2(3, 1)
+    back_z2(1, 1)
+    back_z2(1, 0)
+    back_z1(3, 1)
+    back_z1(2, 0)
+    back_y2(0, 1)
+    back_z2(0, 0)
     resp_x2()
-    back_y1(0, 1)
-    back_z1(1, 1)
-    back_z1(0, 0)
-    z2(2, 0)
+    back_z2(2, 1)
     back_z2(3, 0)
-    back_z1(1, 0)
-    back_z2(2, 1)
-    back_y2(0, 1)
-    back_z1(3, 1)
-    back_z2(1, 1)
-    back_z2(0, 0)
+    back_y1(1, 1)
+    back_y1(1, 0)
+    back_z2(3, 1)
+    result(0, 1)
+    back_z2(2, 0)
+    back_y1(0, 0)
+    back_y1(2, 1)
+    back_y1(3, 0)
+    back_y2(1, 1)
     resp_z()
-    back_y1(3, 0)
-    back_z1(2, 0)
+    back_y2(1, 0)
+    back_y1(3, 1)
+    back_y1(2, 0)
     feature_odd()
-    back_y1(1, 1)
-    back_y1(2, 1)
-    result(0, 1)
+    back_y2(0, 0)
     back_y2(3, 0)
-    back_y1(0, 0)
-    back_z2(3, 1)
-    back_z2(1, 0)
+    back_y2(2, 1)
+    result(1, 1)
+    result(1, 0)
+    back_y2(3, 1)
     resp_result()
-    back_y2(1, 1)
-    back_z2(2, 0)
-    back_y2(2, 1)
-    back_y1(3, 1)
-    back_y1(1, 0)
+    back_y2(2, 0)
+    result(0, 0)
+    result(2, 1)
     result(3, 0)
-    back_y2(0, 0)
-    result(1, 1)
-    back_y1(2, 0)
-    result(2, 1)
-    back_y2(3, 1)
-    back_y2(1, 0)
-    result(0, 0)
-    back_y2(2, 0)
     result(3, 1)
-    result(1, 0)
     result(2, 0)
     for copy in copies:
         copy.wait_send()
@@ -564,15 +564,20 @@
         copy.wait()
 
 
-def finish(resp_in, fgrad_in, kgrad_in, resp, fgrad, kgrad, sem):
-    copies = [
-        pltpu.make_async_copy(kgrad_in, kgrad, sem.at[0]),
-        pltpu.make_async_copy(fgrad_in, fgrad, sem.at[1]),
-        pltpu.make_async_copy(resp_in, resp, sem.at[2]),
-    ]
-    for copy in copies:
+def finish(resp_in, fgrad_in, kgrad_in, resp, fgrad, kgrad, resp_v, fgrad_v, kgrad_v, sem):
+    parts = [(kgrad_in, kgrad_v, kgrad, pl.ds(216 * n, 216)) for n in range(4)]
+    parts += [(fgrad_in, fgrad_v, fgrad, pl.ds(16 * n, 16)) for n in range(2)]
+    parts += [(resp_in, resp_v, resp, pl.ds(0, 32))]
+    loads, stores = [], []
+    for n, (source, middle, target, rows) in enumerate(parts):
+        loads.append(pltpu.make_async_copy(source.at[rows], middle.at[rows], sem.at[0, n]))
+        stores.append(pltpu.make_async_copy(middle.at[rows], target.at[rows], sem.at[1, n]))
+    for copy in loads:
         copy.start()
-    for copy in copies:
+    for load, store in zip(loads, stores):
+        load.wait()
+        store.start()
+    for copy in stores:
         copy.wait()
 
 
@@ -630,7 +635,12 @@
         out_shape=results,
         in_specs=[hbm] * 3,
         out_specs=(hbm,) * 3,
-        scratch_shapes=[pltpu.SemaphoreType.DMA((3,))],
+        scratch_shapes=[
+            pltpu.VMEM((32, 1024), BF16),
+            pltpu.VMEM((32, 2, 4096), BF16),
+            pltpu.VMEM((864, 512), F32),
+            pltpu.SemaphoreType.DMA((2, 7)),
+        ],
         compiler_params=pltpu.CompilerParams(vmem_limit_bytes=VMEM_MIB * 2**20),
     )(*parts)
     return (

time: 139 us -> 65.9 us (0.47)
  Pallas kernels: 137 us -> 64.2 us
    pallas_call x1, Pallas kernels: 72.6 us -> 2.52 us  [on_device(): pl.pallas_call(finish, out_shape=results, in_specs=[hbm] * 3, out_specs=(...]
    pallas_call x1, Pallas kernels: 64.6 us -> 61.7 us  [on_device(): pl.pallas_call(kernel, out_shape=results, in_specs=[hbm] * 3, out_specs=(...]
where the time goes in v5:
time: 65.9 us; the launch traced here: 64.9 us
  Pallas kernels  64.2 us (97%)
    pallas_call x1, Pallas kernels, on_device(): pl.pallas_call(kernel, out_shape=results, in_specs=[hbm] * 3, out_specs=(...  61.7 us
    pallas_call x1, Pallas kernels, on_device(): pl.pallas_call(finish, out_shape=results, in_specs=[hbm] * 3, out_specs=(...  2.52 us

profile of v5, /device:TPU:8, one launch (start us, length us, event | category | flops | bytes accessed | tf_op | source)
XLA Modules:
  0.0 64.9 jit_solution(8182240485715379548)
XLA Ops:
  0.6 61.7 %shard_map.58 = (bf16[32,1024]{1,0:T(8,128)(2,1)}, bf16[32,2,4096]{2,1,0:T(2,128)(2,1)}, f32[864,512]{1,0:T(8,128)}) custom-call(bf16[32,2,4096]{2,1,0:T(2,128)(2,1)} %feat_in.1, bf16[864,512]{1,0:T(8,128)(2,1)} %bitcast.8, bf16[32,1024]{1,0:T(8,128)(2,1)} %bitcast.9), custom_call_target="tpu_custom_call" | custom-call | tf_op jit(solution)/shard_map/pallas_call | solution.py:590
  62.4 2.5 %shard_map.59 = (bf16[32,1024]{1,0:T(8,128)(2,1)}, bf16[32,2,4096]{2,1,0:T(2,128)(2,1)}, f32[864,512]{1,0:T(8,128)}) custom-call(bf16[32,1024]{1,0:T(8,128)(2,1)} %get-tuple-element.9.resp_in, bf16[32,2,4096]{2,1,0:T(2,128)(2,1)} %get-tuple-element.10.fgrad_in, f32[864,512]{1,0:T(8,128)} %get-tuple-element.11.kgrad_in), custom_call_target="tpu_custom_call" | custom-call | tf_op jit(solution)/shard_map/pallas_call | solution.py:633

commit v6 on v5

--- a/solution.py
+++ b/solution.py
@@ -91,13 +91,6 @@
     load_feat.start()
     load_kern.start()
 
-    lane_in = lax.broadcasted_iota(jnp.int32, (512, 512), 0)
-    lane_out = lax.broadcasted_iota(jnp.int32, (512, 512), 1)
-    target = (
-        ((lane_in >> 6) & 1) * 256 + (lane_in & 1) * 128
-        + (lane_in >> 7) * 32 + ((lane_in & 63) >> 1)
-    )
-    perm[...] = jnp.where(target == lane_out, 1.0, 0.0).astype(BF16)
     pl.semaphore_wait(barrier, len(partners))
 
     copies = []
@@ -182,6 +175,15 @@
     def next_wait():
         for name in ("own_core", "near_core", "far_core", "opp_core"):
             moves[name].wait_recv()
+
+    def sort_table():
+        lane_in = lax.broadcasted_iota(jnp.int32, (512, 512), 0)
+        lane_out = lax.broadcasted_iota(jnp.int32, (512, 512), 1)
+        target = (
+            ((lane_in >> 6) & 1) * 256 + (lane_in & 1) * 128
+            + (lane_in >> 7) * 32 + ((lane_in & 63) >> 1)
+        )
+        perm[...] = jnp.where(target == lane_out, 1.0, 0.0).astype(BF16)
 
     def split_cells(plane):
         rows = feat[:, plane, :]
@@ -464,6 +466,7 @@
         keep(fgrad, fgrad_out)
 
     cot_start()
+    sort_table()
     feat_odd()
     feat_even()
     cot_z()

time: 65.9 us -> 66.1 us (level)
  no operation moved by 1% of the time
where the time goes in v6:
time: 66.1 us; the launch traced here: 65 us
  Pallas kernels  64.3 us (97%)
    pallas_call x1, Pallas kernels, on_device(): pl.pallas_call(kernel, out_shape=results, in_specs=[hbm] * 3, out_specs=(...  61.8 us
    pallas_call x1, Pallas kernels, on_device(): pl.pallas_call(finish, out_shape=results, in_specs=[hbm] * 3, out_specs=(...  2.52 us

profile of v6, /device:TPU:8, one launch (start us, length us, event | category | flops | bytes accessed | tf_op | source)
XLA Modules:
  0.0 65.0 jit_solution(4288495432226639879)
XLA Ops:
  0.6 61.8 %shard_map.58 = (bf16[32,1024]{1,0:T(8,128)(2,1)}, bf16[32,2,4096]{2,1,0:T(2,128)(2,1)}, f32[864,512]{1,0:T(8,128)}) custom-call(bf16[32,2,4096]{2,1,0:T(2,128)(2,1)} %feat_in.1, bf16[864,512]{1,0:T(8,128)(2,1)} %bitcast.8, bf16[32,1024]{1,0:T(8,128)(2,1)} %bitcast.9), custom_call_target="tpu_custom_call" | custom-call | tf_op jit(solution)/shard_map/pallas_call | solution.py:593
  62.4 2.5 %shard_map.59 = (bf16[32,1024]{1,0:T(8,128)(2,1)}, bf16[32,2,4096]{2,1,0:T(2,128)(2,1)}, f32[864,512]{1,0:T(8,128)}) custom-call(bf16[32,1024]{1,0:T(8,128)(2,1)} %get-tuple-element.9.resp_in, bf16[32,2,4096]{2,1,0:T(2,128)(2,1)} %get-tuple-element.10.fgrad_in, f32[864,512]{1,0:T(8,128)} %get-tuple-element.11.kgrad_in), custom_call_target="tpu_custom_call" | custom-call | tf_op jit(solution)/shard_map/pallas_call | solution.py:636

commit v7 on v6

--- a/solution.py
+++ b/solution.py
@@ -568,7 +568,7 @@
 
 
 def finish(resp_in, fgrad_in, kgrad_in, resp, fgrad, kgrad, resp_v, fgrad_v, kgrad_v, sem):
-    parts = [(kgrad_in, kgrad_v, kgrad, pl.ds(216 * n, 216)) for n in range(4)]
+    parts = [(kgrad_in, kgrad_v, kgrad, pl.ds(96 * n, 96)) for n in range(9)]
     parts += [(fgrad_in, fgrad_v, fgrad, pl.ds(16 * n, 16)) for n in range(2)]
     parts += [(resp_in, resp_v, resp, pl.ds(0, 32))]
     loads, stores = [], []
@@ -642,7 +642,7 @@
             pltpu.VMEM((32, 1024), BF16),
             pltpu.VMEM((32, 2, 4096), BF16),
             pltpu.VMEM((864, 512), F32),
-            pltpu.SemaphoreType.DMA((2, 7)),
+            pltpu.SemaphoreType.DMA((2, 12)),
         ],
         compiler_params=pltpu.CompilerParams(vmem_limit_bytes=VMEM_MIB * 2**20),
     )(*parts)

time: 66.1 us -> 66.2 us (level)
  no operation moved by 1% of the time
where the time goes in v7:
time: 66.2 us; the launch traced here: 65.1 us
  Pallas kernels  64.4 us (97%)
    pallas_call x1, Pallas kernels, on_device(): pl.pallas_call(kernel, out_shape=results, in_specs=[hbm] * 3, out_specs=(...  61.8 us
    pallas_call x1, Pallas kernels, on_device(): pl.pallas_call(finish, out_shape=results, in_specs=[hbm] * 3, out_specs=(...  2.62 us

profile of v7, /device:TPU:8, one launch (start us, length us, event | category | flops | bytes accessed | tf_op | source)
XLA Modules:
  0.0 65.1 jit_solution(2499789050690809360)
XLA Ops:
  0.6 61.8 %shard_map.58 = (bf16[32,1024]{1,0:T(8,128)(2,1)}, bf16[32,2,4096]{2,1,0:T(2,128)(2,1)}, f32[864,512]{1,0:T(8,128)}) custom-call(bf16[32,2,4096]{2,1,0:T(2,128)(2,1)} %feat_in.1, bf16[864,512]{1,0:T(8,128)(2,1)} %bitcast.8, bf16[32,1024]{1,0:T(8,128)(2,1)} %bitcast.9), custom_call_target="tpu_custom_call" | custom-call | tf_op jit(solution)/shard_map/pallas_call | solution.py:593
  62.4 2.6 %shard_map.59 = (bf16[32,1024]{1,0:T(8,128)(2,1)}, bf16[32,2,4096]{2,1,0:T(2,128)(2,1)}, f32[864,512]{1,0:T(8,128)}) custom-call(bf16[32,1024]{1,0:T(8,128)(2,1)} %get-tuple-element.9.resp_in, bf16[32,2,4096]{2,1,0:T(2,128)(2,1)} %get-tuple-element.10.fgrad_in, f32[864,512]{1,0:T(8,128)} %get-tuple-element.11.kgrad_in), custom_call_target="tpu_custom_call" | custom-call | tf_op jit(solution)/shard_map/pallas_call | solution.py:636
